TPU v7x, 256 devices: a whole 4x4x8 slice. The times are simulated.
256 devices in a mesh: sta: 8 (over z), win: 32 (over y, x, core).
Axes of the slice: x: 4, y: 4, z: 8, core: 2. Of those that a mesh axis runs over, the one named last changes fastest.
Arguments:
- traces: float32 [1024, 32, 8192], P('sta', 'win')
- pair_blocks: int32 [8, 2], P('sta'), may hold values from 0 to 15, as said below
Outputs:
- correlations: float32 [64, 8, 64, 512], P('win', 'sta')
Inputs may be any that keep to these rules, and one draw needn't show every extreme that they name: pair_blocks[p, 0] <= pair_blocks[p, 1] <= pair_blocks[p, 0] + 2; pairs per first block are uneven.
All inputs are finite; a program needn't handle non-finite values.
Results may differ from a plain program's by a relative error of at most 0.0017.
Values may be sent and summed in bfloat16 or wider, within the bound.
A program may use at most 64 MiB of HBM per device.

v0:
```python
import math

import jax
import jax.numpy as jnp
from jax import lax
from jax.sharding import PartitionSpec as P

BLOCK = 64
LAGS = 512
K0 = 256
BAND_DEV = 16


def lag_tables(first_bin, count, length, lags):
    freqs = first_bin + jnp.arange(count, dtype=jnp.int32)
    shifts = (jnp.arange(lags, dtype=jnp.int32) - lags // 2) % length
    phase = freqs[:, None] * shifts[None, :] % length
    angle = phase.astype(jnp.float32) * (2.0 * math.pi / length)
    return (jnp.cos(angle), jnp.sin(angle))


def to_lags(cross_re, cross_im, cos_table, sin_table, norm):
    lagged = jnp.einsum("pfij,ft->ipjt", cross_re, cos_table, precision=lax.Precision.HIGHEST)
    lagged = lagged - jnp.einsum(
        "pfij,ft->ipjt", cross_im, sin_table, precision=lax.Precision.HIGHEST
    )
    return lagged * norm


def body(traces, pair_blocks):
    num_win = lax.axis_size("win")
    sta_dev, win_dev, length = traces.shape
    nbins = BAND_DEV * num_win
    step = math.gcd(nbins, 256)
    flat = jnp.transpose(traces, (1, 0, 2)).reshape(win_dev * sta_dev, length)
    sample_idx = lax.broadcasted_iota(jnp.int32, (length, step), 0)
    pieces = []
    for first in range(0, nbins, step):
        freq = lax.broadcasted_iota(jnp.int32, (length, step), 1) + (K0 + first)
        angle = (sample_idx * freq % length).astype(jnp.float32) * (2.0 * math.pi / length)
        table = jnp.concatenate([jnp.cos(angle), -jnp.sin(angle)], axis=1)
        result = lax.dot_general(
            table,
            flat,
            (((0,), (1,)), ((), ())),
            precision=lax.Precision.HIGHEST,
            preferred_element_type=jnp.float32,
        )
        pieces.append(result.reshape(2, step, win_dev, sta_dev))
    spectrum = jnp.transpose(jnp.concatenate(pieces, axis=1), (0, 2, 1, 3))
    power = jnp.mean(spectrum[0] * spectrum[0] + spectrum[1] * spectrum[1], axis=1, keepdims=True)
    scale = jnp.sqrt(power + 1e-06)
    white = (spectrum / scale[None]).astype(jnp.bfloat16)
    banded = lax.all_to_all(white, "win", split_axis=2, concat_axis=1, tiled=True)
    everyone = lax.all_gather(banded, "sta", axis=3, tiled=True)
    windows = everyone.shape[1]
    norm = float(windows * nbins) ** (-0.5)

    def block_of(block_id):
        sliced = lax.dynamic_slice_in_dim(everyone, block_id * BLOCK, BLOCK, 3)
        return jnp.concatenate([sliced[0], sliced[1]], axis=-1)

    left = block_of(pair_blocks[0, 0])
    right = block_of(pair_blocks[0, 1])
    prod = jnp.einsum("wfa,wfb->fab", left, right, preferred_element_type=jnp.float32)
    real_list = [prod[:, :BLOCK, :BLOCK] + prod[:, BLOCK:, BLOCK:]]
    imag_list = [prod[:, BLOCK:, :BLOCK] - prod[:, :BLOCK, BLOCK:]]
    cross_re = jnp.stack(real_list)
    cross_im = jnp.stack(imag_list)
    band_start = K0 + lax.axis_index("win") * BAND_DEV
    cos_table, sin_table = lag_tables(band_start, BAND_DEV, length, LAGS)
    return lax.psum_scatter(
        to_lags(cross_re, cross_im, cos_table, sin_table, norm),
        "win",
        scatter_dimension=0,
        tiled=True,
    )


def solution(mesh):
    in_specs = (P("sta", "win", None), P("sta", None))
    out_specs = P("win", "sta", None, None)
    return jax.shard_map(body, mesh=mesh, in_specs=in_specs, out_specs=out_specs, check_vma=False)
```

profile of v0, /device:TPU:1, one launch (start us, length us, event | category | flops | bytes accessed | tf_op | source)
XLA Modules:
  0.0 304.7 jit_solution(6856016216639964006)
XLA Ops:
  6.5 0.0 all-gather.2.cloned.1.call-start
  6.5 37.1 %fusion.17 = (f32[8192,256]{0,1:T(8,128)}, f32[8192,256]{0,1:T(8,128)}) fusion(s32[256]{0:T(256)S(1)} %iota_add_fusion.1), kind=kLoop, calls=%fused_computation.28 | loop fusion | flops 31457280 | bytes 16778240 | tf_op jit(solution)/shard_map/cos | solution.py:41
  43.7 33.0 %fusion.16 = (f32[8192,256]{0,1:T(8,128)S(1)}, f32[8192,256]{0,1:T(8,128)S(1)}) fusion(s32[256]{0:T(256)S(1)} %iota_add_fusion), kind=kLoop, calls=%fused_computation.27 | loop fusion | flops 31457280 | bytes 16778240 | tf_op jit(solution)/shard_map/cos | solution.py:41
  76.7 6.9 %pad_maximum_fusion = f32[8192,512]{0,1:T(8,128)S(1)} fusion(f32[8192,256]{0,1:T(8,128)} %get-tuple-element.12, f32[8192,256]{0,1:T(8,128)} %get-tuple-element.11), kind=kLoop, calls=%fused_computation | loop fusion | flops 4194304 | bytes 33554432 | tf_op jit(solution)/shard_map/concatenate | solution.py:41
  83.6 15.5 %fusion.20 = f32[2,256,1,128]{3,1,0,2:T(8,128)S(1)} fusion(f32[2,256,8192]{2,1,0:T(8,128)S(1)} %bitcast.49, f32[128,1,8192]{2,1,0:T(1,128)} %param.2), kind=kOutput, calls=%fused_computation.31 | convolution fusion | flops 6442450944 | bytes 21233664 | tf_op jit(solution)/shard_map/dot_general | solution.py:42
  99.1 2.0 pad_maximum_fusion.1
  101.2 0.0 copy-start
  101.2 15.3 %fusion.23 = f32[2,256,1,128]{3,1,0,2:T(8,128)S(1)} fusion(f32[2,256,8192]{2,1,0:T(8,128)S(1)} %bitcast.50, f32[128,1,8192]{2,1,0:T(1,128)} %param.2), kind=kOutput, calls=%fused_computation.32 | convolution fusion | flops 6442450944 | bytes 21233664 | tf_op jit(solution)/shard_map/dot_general | solution.py:42
  116.5 0.1 fusion.35
  116.6 0.1 fusion.31
  116.7 0.3 copy.11
  117.0 17.3 %all_to_all.12 = bf16[2,1,512,128]{3,0,1,2:T(2,128)(2,1)S(1)} all-to-all(bf16[2,1,512,128]{3,0,1,2:T(2,128)(2,1)S(1)} %copy.11), channel_id=1, replica_groups=mesh['sta'=8,'win'=32] {'win'}, dimensions={2} | all-to-all | bytes 524288 | tf_op jit(solution)/shard_map/all_to_all | solution.py:54
  134.2 0.8 copy.13
  135.0 0.0 all-gather.2.cloned.1.call-update
  135.1 0.3 reduce-scatter.2.cloned.1.call-start
  135.3 0.0 copy-done
  135.4 0.6 fusion.64
  137.4 40.4 %all-gather.2.cloned.1.call-done = bf16[2,32,16,1024]{3,1,2,0:T(8,128)(2,1)} async-done(((bf16[2,32,16,128]{3,1,2,0:T(8,128)(2,1)}), bf16[2,32,16,1024]{3,1,2,0:T(8,128)(2,1)}) %all-gather.2.cloned.1.call-update) | async-done | bytes 2097168 | tf_op jit(solution)/shard_map/all_gather | solution.py:55
  177.7 1.3 dynamic-slice_bitcast_fusion.1
  179.1 0.5 fusion.38
  179.6 0.3 slice_subtract_fusion
  180.0 6.9 %fusion.29 = f32[512,64,64]{0,2,1:T(8,128)S(1)} fusion(f32[16,64,64]{2,1,0:T(8,128)S(1)} %get-tuple-element.10, s32[512]{0:T(512)S(1)} %add_select_fusion.3, s32[16]{0:T(128)S(1)} %iota_add_fusion.2), kind=kOutput, calls=%fused_computation.43 | convolution fusion | flops 402767872 | bytes 8652864 | tf_op jit(solution)/shard_map/pfij,ft->ipjt/dot_general | solution.py:23
  186.8 9.4 %multiply_bitcast_fusion = f32[64,1,64,512]{3,2,0,1:T(8,128)} fusion(f32[512,64,64]{0,2,1:T(8,128)S(1)} %fusion.29, f32[16,64,64]{2,1,0:T(8,128)S(1)} %get-tuple-element.9, s32[512]{0:T(512)S(1)} %add_select_fusion.3, s32[16]{0:T(128)S(1)} %iota_add_fusion.2), kind=kOutput, calls=%fused_computation.14 | convolution fusion | flops 406962176 | bytes 17041472 | tf_op jit(solution)/shard_map/pfij,ft->ipjt/dot_general | solution.py:24
  196.2 0.0 reduce-scatter.2.cloned.1.call-update
  196.2 101.7 %reduce-scatter.2.cloned.1.call-done = f32[2,1,64,512]{3,2,0,1:T(8,128)} async-done(((f32[64,1,64,512]{3,2,0,1:T(8,128)}), f32[2,1,64,512]{3,2,0,1:T(8,128)}) %reduce-scatter.2.cloned.1.call-update) | async-done | bytes 262160 | tf_op jit(solution)/shard_map/reduce_scatter | solution.py:72
  (5 shorter events, 0.0 us)
Async XLA Ops:
  6.5 171.2 %all-gather.2.cloned.1.call-start = ((), (), s32[]{:S(2)}) async-start(), calls=%async_computation.2 | async-start | bytes 2359296 | tf_op jit(solution)/shard_map/all_gather | solution.py:55
  101.2 34.2 %copy-start = (s32[1,2]{1,0:T(1,128)S(1)}, s32[1,2]{1,0:T(1,128)}, u32[]{:S(2)}) copy-start(s32[1,2]{1,0:T(1,128)} %param.3) | copy-start | bytes 28
  135.1 162.8 %reduce-scatter.2.cloned.1.call-start = ((), (), s32[]{:S(2)}) async-start(), calls=%async_computation.3 | async-start | bytes 8650752 | tf_op jit(solution)/shard_map/reduce_scatter | solution.py:72
Sparse Core Ops, SparseCore 0:
  135.2 42.5 all-gather.1
  196.3 101.5 reduce-scatter.1
where the time goes:
time: 305 us
  waiting for transfers between devices  142 us (47%)
  other arithmetic  79.6 us (26%)
  matrix products  47.6 us (16%)
  blocking collectives  17.3 us (6%)
  between operations  14.8 us (5%)
    reduce_scatter x1, waiting for transfers between devices, body(): lax.psum_scatter(to_lags(cross_re, cross_im, cos_table, sin_table, norm),...  102 us
    cos x2, other arithmetic, body(): table = jnp.concatenate([jnp.cos(angle), -jnp.sin(angle)], axis=1)  70.2 us
    all_gather x1, waiting for transfers between devices, body(): everyone = lax.all_gather(banded, 'sta', axis=3, tiled=True)  40.4 us
    dot_general x2, matrix products, body(): lax.dot_general(table, flat, (((0,), (1,)), ((), ())), precision=lax.Prec...  30.9 us
    all_to_all x1, blocking collectives, body(): lax.all_to_all(white, 'win', split_axis=2, concat_axis=1, tiled=True)  17.3 us
    dot_general x1, matrix products, to_lags(): jnp.einsum('pfij,ft->ipjt', cross_im, sin_table, precision=lax.Precision....  9.35 us
    concatenate x2, other arithmetic, body(): table = jnp.concatenate([jnp.cos(angle), -jnp.sin(angle)], axis=1)  8.91 us
    dot_general x1, matrix products, to_lags(): jnp.einsum('pfij,ft->ipjt', cross_re, cos_table, precision=lax.Precision....  6.85 us
  transfers between devices with their start and end apart: 2, of which 2 were waited for; matrix products, arithmetic and copies ran while one was open for 0% of the time, Pallas kernels for 0%

commit v1 on v0

v1 whole, which is shorter than its diff:
```python
import functools
import math

import jax
import jax.numpy as jnp
import ml_dtypes
import numpy as np
from jax import lax
from jax.experimental import pallas as pl
from jax.experimental.pallas import tpu as pltpu
from jax.sharding import PartitionSpec as P

L = 8192
LAGS = 512
K0 = 256
BANDS = 512
STA = 8
WIN = 32
ST = 128
SEG = 64
RADIX = 16
FOLD = L // RADIX
MESH = pl.DeviceIdType.MESH


def bin_of():
    bins = np.zeros((WIN, STA, 2), np.int64)
    for z in range(STA):
        for q in range(1, 8):
            for u in range(4):
                m = 16 + 4 * z + u
                bins[4 * (q - 1) + u, z] = (16 * m + q, 16 * m + 16 - q)
        for half in range(2):
            for u in range(2):
                for s in range(2):
                    bins[28 + 2 * half + u, z, s] = 16 * (16 + 4 * z + 2 * u + s) + 8 * half
    return bins


def split(table):
    high = table.astype(ml_dtypes.bfloat16)
    low = (table - high.astype(np.float64)).astype(ml_dtypes.bfloat16)
    return high, low


@functools.cache
def tables():
    bins = bin_of()
    n = np.arange(FOLD)

    def trig(k):
        angle = 2 * math.pi * ((k * n) % L) / L
        return np.cos(angle), np.sin(angle)

    odd = np.zeros((7, 4, STA, 2, 2, 2 * FOLD))
    for q in range(1, 8):
        for u in range(4):
            for z in range(STA):
                for s in range(2):
                    c, d = trig(bins[4 * (q - 1) + u, z, s])
                    sign = 1.0 if s == 0 else -1.0
                    odd[q - 1, u, z, s, 0] = np.concatenate([c, sign * d])
                    odd[q - 1, u, z, s, 1] = np.concatenate([-d, sign * c])
    even = np.zeros((2, 2, STA, 2, 2, FOLD))
    for half in range(2):
        for u in range(2):
            for z in range(STA):
                for s in range(2):
                    c, d = trig(bins[28 + 2 * half + u, z, s])
                    even[half, u, z, s, 0] = c
                    even[half, u, z, s, 1] = -d
    shifts = (np.arange(LAGS) - LAGS // 2) % L
    angle = 2 * math.pi * ((bins[..., None] * shifts) % L) / L
    lag = np.stack([np.cos(angle), -np.sin(angle)], axis=3)
    lag = lag.reshape(2 * BANDS, LAGS).T * float(WIN * BANDS) ** (-0.5)
    odd = np.stack(split(odd.reshape(7, 128, 2 * FOLD)), axis=1)
    even = np.stack(split(even.reshape(2, 64, FOLD)), axis=1)
    lag = np.concatenate(split(lag), axis=0)
    return odd, even, lag


def fold16(x):
    r2 = math.sqrt(0.5)
    c1 = math.cos(math.pi / 8)
    c3 = math.sin(math.pi / 8)
    e = [x[a] + x[a + 8] for a in range(8)]
    o = [x[a] - x[a + 8] for a in range(8)]
    f = [e[a] + e[a + 4] for a in range(4)]
    g = [e[a] - e[a + 4] for a in range(4)]
    f02, f13 = f[0] + f[2], f[1] + f[3]
    gd, gs = r2 * (g[1] - g[3]), r2 * (g[1] + g[3])
    d = [None] + [o[a] - o[8 - a] for a in range(1, 4)]
    s = [None] + [o[a] + o[8 - a] for a in range(1, 4)]
    d2, s2 = r2 * d[2], r2 * s[2]
    p, m = o[0] + d2, o[0] - d2
    u, v = c1 * d[1] + c3 * d[3], c3 * d[1] - c1 * d[3]
    pp, mm = s2 + o[4], s2 - o[4]
    uu, vv = c3 * s[1] + c1 * s[3], c1 * s[1] - c3 * s[3]
    real = [f02 + f13, p + u, g[0] + gd, m + v, f[0] - f[2], m - v, g[0] - gd, p - u, f02 - f13]
    imag = [None, -(uu + pp), -(g[2] + gs), -(vv + mm), f[3] - f[1], mm - vv, g[2] - gs, pp - uu]
    return real, imag


def kernel(
    x_ref, pair_ref, odd_ref, even_ref, lag_ref, out_ref,
    x_v, odd_v, even_v, lag_v, pairs, fodd, feven, spec,
    asend, arecv, bsend, brecv, csend, crecv, dsend, drecv, order,
    x_sem, t_sem, p_ssem, p_rsem, a_ssem, a_rsem, b_ssem, b_rsem, c_ssem, c_rsem, d_ssem, d_rsem,
):
    me_s = lax.axis_index("sta")
    me_w = lax.axis_index("win")

    x_copies = [
        pltpu.make_async_copy(x_ref.at[pl.ds(2048 * i, 2048)], x_v.at[pl.ds(2048 * i, 2048)], x_sem.at[i])
        for i in range(4)
    ]
    t_copies = [
        pltpu.make_async_copy(src, dst, t_sem.at[i])
        for i, (src, dst) in enumerate(((odd_ref, odd_v), (even_ref, even_v), (lag_ref, lag_v)))
    ]
    for copy in x_copies + t_copies:
        copy.start()

    barrier = pltpu.get_barrier_semaphore()

    def greet(axis, me, count):
        def step(i, _):
            peer = lax.rem(me + i, count)
            pl.semaphore_signal(barrier, inc=1, device_id={axis: peer}, device_id_type=MESH)
            return 0

        lax.fori_loop(1, count, step, 0)

    greet("sta", me_s, STA)
    greet("win", me_w, WIN)

    for chunk in range(4):
        x_copies[chunk].wait()

        def fold(t, _, chunk=chunk):
            lane_tile = lax.rem(t, 4)
            i2 = t // 4
            first = chunk * 2048 + i2 * 64
            x = [x_v[pl.ds(first + 4 * a + lane_tile, 16, stride=128), :] for a in range(RADIX)]
            real, imag = fold16(x)
            row = pl.multiple_of((chunk // 2) * 64 + i2 * 32 + (chunk % 2) * 16, 16)
            lane = pl.multiple_of(lane_tile * 128, 128)

            def put(dst, at, value):
                high = value.astype(jnp.bfloat16)
                low = (value - high.astype(jnp.float32)).astype(jnp.bfloat16)
                dst[pl.ds(row, 16), pl.ds(at, 128)] = high
                dst[pl.ds(row + 128, 16), pl.ds(at, 128)] = low

            put(feven.at[0], lane, real[0])
            put(feven.at[1], lane, real[8])
            for q in range(1, 8):
                put(fodd.at[q - 1], lane, real[q])
                put(fodd.at[q - 1], pl.multiple_of(lane + FOLD, 128), imag[q])
            return 0

        lax.fori_loop(0, 8, fold, 0)

    contract_last = (((1,), (1,)), ((), ()))

    def dft(table, data):
        high = lax.dot_general(table[0], data, contract_last, preferred_element_type=jnp.float32)
        low = lax.dot_general(table[1], data[:ST], contract_last, preferred_element_type=jnp.float32)
        return high[:, :ST] + (high[:, ST:] + low)

    t_copies[0].wait()

    def odd_class(q, power):
        value = dft(odd_v[q], fodd[q])
        spec[pl.ds(pl.multiple_of(q * 128, 128), 128), :] = value
        return power + jnp.sum((value * value).reshape(16, 8, ST), axis=0)

    power = lax.fori_loop(0, 7, odd_class, jnp.zeros((8, ST), jnp.float32))
    t_copies[1].wait()
    for half in range(2):
        value = dft(even_v[half], feven[half])
        spec[896 + 64 * half : 960 + 64 * half, :] = value
        power = power + jnp.sum((value * value).reshape(8, 8, ST), axis=0)
    mean = jnp.sum(power, axis=0, keepdims=True) * (1.0 / BANDS)
    inverse = 1.0 / jnp.sqrt(mean + 1e-06)
    for i in range(WIN):
        asend[i] = (spec[32 * i : 32 * i + 32, :] * inverse).astype(jnp.bfloat16)

    pl.semaphore_wait(barrier, STA - 1 + WIN - 1)

    def p_copy(peer, slot):
        return pltpu.make_async_remote_copy(
            src_ref=pair_ref, dst_ref=pairs.at[slot], send_sem=p_ssem.at[peer], recv_sem=p_rsem.at[slot],
            device_id={"sta": peer}, device_id_type=MESH,
        )

    def a_copy(peer, slot):
        return pltpu.make_async_remote_copy(
            src_ref=asend.at[peer], dst_ref=arecv.at[slot], send_sem=a_ssem.at[peer], recv_sem=a_rsem.at[slot],
            device_id={"win": peer}, device_id_type=MESH,
        )

    def b_copy(peer, slot):
        return pltpu.make_async_remote_copy(
            src_ref=bsend.at[peer], dst_ref=brecv.at[slot], send_sem=b_ssem.at[peer], recv_sem=b_rsem.at[slot],
            device_id={"sta": peer}, device_id_type=MESH,
        )

    def c_copy(peer, slot):
        return pltpu.make_async_remote_copy(
            src_ref=csend.at[peer], dst_ref=crecv.at[slot], send_sem=c_ssem.at[peer], recv_sem=c_rsem.at[slot],
            device_id={"sta": peer}, device_id_type=MESH,
        )

    def d_copy(peer, slot):
        return pltpu.make_async_remote_copy(
            src_ref=dsend.at[peer], dst_ref=drecv.at[slot], send_sem=d_ssem.at[peer], recv_sem=d_rsem.at[slot],
            device_id={"win": peer}, device_id_type=MESH,
        )

    def each(count, me, action):
        def step(i, _):
            action(lax.rem(me + i, count))
            return 0

        lax.fori_loop(1, count, step, 0)

    each(WIN, me_w, lambda peer: a_copy(peer, me_w).start())
    each(STA, me_s, lambda peer: p_copy(peer, me_s).start())
    arecv[me_w] = asend[me_w]
    pairs[me_s, 0, 0] = pair_ref[0, 0]
    pairs[me_s, 0, 1] = pair_ref[0, 1]
    each(WIN, me_w, lambda peer: a_copy(peer, peer).wait_recv())

    for z in range(STA):
        bsend[z] = jnp.swapaxes(arecv[:, 4 * z : 4 * z + 4, :], 0, 1)
    each(STA, me_s, lambda peer: b_copy(peer, me_s).start())
    brecv[me_s] = bsend[me_s]
    each(STA, me_s, lambda peer: b_copy(peer, peer).wait_recv())
    each(STA, me_s, lambda peer: p_copy(peer, peer).wait_recv())

    left_lanes = lax.broadcasted_iota(jnp.int32, (WIN, ST), 1) < 64

    def one_pair(i, _):
        p = lax.rem(me_s + i, STA)
        a = pairs[p, 0, 0]
        b = pairs[p, 0, 1]
        a_odd = lax.rem(a, 2) == 1
        b_odd = lax.rem(b, 2) == 1
        first = brecv[a // 2]
        second = brecv[b // 2].astype(jnp.float32)
        for s in range(2):
            re, im = second[2 * s], second[2 * s + 1]
            re_roll, im_roll = pltpu.roll(re, 64, 1), pltpu.roll(im, 64, 1)
            re_l, im_l = jnp.where(b_odd, re_roll, re), jnp.where(b_odd, im_roll, im)
            re_r, im_r = jnp.where(b_odd, re, re_roll), jnp.where(b_odd, im, im_roll)
            right = jnp.concatenate(
                [jnp.where(left_lanes, re_l, -im_r), jnp.where(left_lanes, im_l, re_r)], axis=0
            ).astype(jnp.bfloat16)
            left = first[2 * s : 2 * s + 2].reshape(2 * WIN, ST)
            prod = lax.dot_general(left, right, (((0,), (0,)), ((), ())), preferred_element_type=jnp.float32)
            prod = jnp.where(a_odd, prod[64:], prod[:64])
            top, low = prod[:32], prod[32:]
            csend[p, 64 * s : 64 * s + 32, :] = jnp.where(left_lanes, top, pltpu.roll(low, 64, 1))
            csend[p, 64 * s + 32 : 64 * s + 64, :] = jnp.where(left_lanes, pltpu.roll(top, 64, 1), low)

        @pl.when(i < STA)
        def _():
            c_copy(p, me_s).start()

        return 0

    lax.fori_loop(1, STA + 1, one_pair, 0)
    crecv[me_s] = csend[me_s]
    each(STA, me_s, lambda peer: c_copy(peer, peer).wait_recv())

    for w in range(WIN):
        for z in range(STA):
            dsend[w, 4 * z : 4 * z + 4, :] = crecv[z, pl.ds(w, 4, stride=32), :]
    each(WIN, me_w, lambda peer: d_copy(peer, me_w).start())
    drecv[me_w] = dsend[me_w]
    t_copies[2].wait()
    each(WIN, me_w, lambda peer: d_copy(peer, peer).wait_recv())

    cross = drecv[...].reshape(WIN * 32, ST)
    high = cross.astype(jnp.bfloat16)
    low = (cross - high.astype(jnp.float32)).astype(jnp.bfloat16)
    both = jnp.concatenate([high, low], axis=1)

    def lags(t, _):
        row = pl.multiple_of(t * 128, 128)
        value = jnp.dot(lag_v[pl.ds(row, 128), :], both, preferred_element_type=jnp.float32)
        extra = jnp.dot(lag_v[pl.ds(row + LAGS, 128), :], high, preferred_element_type=jnp.float32)
        value = jnp.transpose(value[:, :ST] + (value[:, ST:] + extra))
        for i2 in range(2):
            for j2 in range(2):
                part = value[(2 * i2 + j2) * 32 : (2 * i2 + j2) * 32 + 32]
                order[pl.ds(i2 * 64 + j2, 32, stride=2), :] = part
        out_ref[:, :, pl.ds(row, 128)] = order[...].reshape(2, 64, 128)
        return 0

    lax.fori_loop(0, LAGS // 128, lags, 0)

    each(WIN, me_w, lambda peer: a_copy(peer, me_w).wait_send())
    each(STA, me_s, lambda peer: p_copy(peer, me_s).wait_send())
    each(STA, me_s, lambda peer: b_copy(peer, me_s).wait_send())
    each(STA, me_s, lambda peer: c_copy(peer, me_s).wait_send())
    each(WIN, me_w, lambda peer: d_copy(peer, me_w).wait_send())


def body(traces, pair_blocks):
    odd, even, lag = (jnp.asarray(t) for t in tables())
    f32, bf16 = jnp.float32, jnp.bfloat16
    hbm = pl.BlockSpec(memory_space=pl.ANY)
    out = pl.pallas_call(
        kernel,
        out_shape=jax.ShapeDtypeStruct((2, 64, LAGS), f32),
        in_specs=[hbm, pl.BlockSpec(memory_space=pltpu.SMEM), hbm, hbm, hbm],
        out_specs=pl.BlockSpec(memory_space=pltpu.VMEM),
        scratch_shapes=[
            pltpu.VMEM((ST * SEG, 128), f32),
            pltpu.VMEM(odd.shape, bf16),
            pltpu.VMEM(even.shape, bf16),
            pltpu.VMEM(lag.shape, bf16),
            pltpu.SMEM((STA, 1, 2), jnp.int32),
            pltpu.VMEM((7, 2 * ST, 2 * FOLD), bf16),
            pltpu.VMEM((2, 2 * ST, FOLD), bf16),
            pltpu.VMEM((2 * BANDS, ST), f32),
            pltpu.VMEM((WIN, 32, ST), bf16),
            pltpu.VMEM((WIN, 32, ST), bf16),
            pltpu.VMEM((STA, 4, WIN, ST), bf16),
            pltpu.VMEM((STA, 4, WIN, ST), bf16),
            pltpu.VMEM((STA, 128, ST), f32),
            pltpu.VMEM((STA, 128, ST), f32),
            pltpu.VMEM((WIN, 32, ST), f32),
            pltpu.VMEM((WIN, 32, ST), f32),
            pltpu.VMEM((ST, 128), f32),
            pltpu.SemaphoreType.DMA((4,)),
            pltpu.SemaphoreType.DMA((3,)),
        ]
        + [pltpu.SemaphoreType.DMA((n,)) for n in (STA, STA, WIN, WIN, STA, STA, STA, STA, WIN, WIN)],
        compiler_params=pltpu.CompilerParams(
            collective_id=0, has_side_effects=True, vmem_limit_bytes=48 * 1024 * 1024
        ),
        name="noise_correlation",
    )(traces.reshape(ST * SEG, 128), pair_blocks, odd, even, lag)
    return out.reshape(2, 1, 64, LAGS)


def solution(mesh):
    in_specs = (P("sta", "win", None), P("sta", None))
    out_specs = P("win", "sta", None, None)
    return jax.shard_map(body, mesh=mesh, in_specs=in_specs, out_specs=out_specs, check_vma=False)
```

time: 305 us -> 59.7 us (0.20)
  waiting for transfers between devices: 142 us -> 0 us
  other arithmetic: 79.6 us -> 0 us
  Pallas kernels: 0 us -> 55.7 us
  matrix products: 47.6 us -> 0 us
  blocking collectives: 17.3 us -> 0 us
  between operations: 14.8 us -> 0.01 us
    reduce_scatter x1 -> x0, waiting for transfers between devices: 102 us -> none  [body(): lax.psum_scatter(to_lags(cross_re, cross_im, cos_table, sin_table, norm),...]
    cos x2 -> x0, other arithmetic: 70.2 us -> none  [body(): table = jnp.concatenate([jnp.cos(angle), -jnp.sin(angle)], axis=1)]
    pallas_call x0 -> x1, Pallas kernels: none -> 55.7 us  [body(): pl.pallas_call(kernel, out_shape=jax.ShapeDtypeStruct((2, 64, LAGS), f32)...]
    dot_general x5 -> x0, matrix products: 47.6 us -> none  [the longest x2 30.9 us: body(): lax.dot_general(table, flat, (((0,), (1,)), ((), ())), precision=lax.Prec...]
    all_gather x1 -> x0, waiting for transfers between devices: 40.4 us -> none  [body(): everyone = lax.all_gather(banded, 'sta', axis=3, tiled=True)]
    all_to_all x1 -> x0, blocking collectives: 17.3 us -> none  [body(): lax.all_to_all(white, 'win', split_axis=2, concat_axis=1, tiled=True)]
    concatenate x2 -> x0, other arithmetic: 8.91 us -> none  [body(): table = jnp.concatenate([jnp.cos(angle), -jnp.sin(angle)], axis=1)]
    unnamed x2 -> x7, local copies, waits for them, and re-layouts: 0.01 us -> 3.9 us
  transfers between devices with their start and end apart: 2 -> 0, of which waited for: 2 -> 0; matrix products, arithmetic and copies ran while one was open for 0% -> 0% of each run, Pallas kernels for 0% -> 0%
where the time goes in v1:
time: 59.7 us; the launch traced here: 59.6 us
  Pallas kernels  55.7 us (93%)
  local copies, waits for them, and re-layouts  3.9 us (7%)
    pallas_call x1, Pallas kernels, body(): pl.pallas_call(kernel, out_shape=jax.ShapeDtypeStruct((2, 64, LAGS), f32)...  55.7 us
    unnamed x7, local copies, waits for them, and re-layouts  3.9 us

profile of v1, /device:TPU:1, one launch (start us, length us, event | category | flops | bytes accessed | tf_op | source)
XLA Modules:
  0.0 59.6 jit_solution(5314523818088169545)
XLA Ops:
  0.0 0.0 copy-start
  0.0 1.6 %copy-done = bf16[1024,1024]{1,0:T(8,128)(2,1)S(1)} copy-done((bf16[1024,1024]{1,0:T(8,128)(2,1)S(1)}, bf16[1024,1024]{1,0:T(8,128)(2,1)}, u32[]{:S(2)}) %copy-start) | copy-done | bytes 2097176
  1.6 0.0 copy-start.1
  1.6 0.9 %copy-done.1 = bf16[2,2,64,512]{3,2,1,0:T(8,128)(2,1)S(1)} copy-done((bf16[2,2,64,512]{3,2,1,0:T(8,128)(2,1)S(1)}, bf16[2,2,64,512]{3,2,1,0:T(8,128)(2,1)}, u32[]{:S(2)}) %copy-start.1) | copy-done | bytes 262168
  2.5 0.0 copy-start.2
  2.5 0.7 %copy-done.2 = s32[1,2]{1,0:T(1,128)S(1)} copy-done((s32[1,2]{1,0:T(1,128)S(1)}, s32[1,2]{1,0:T(1,128)}, u32[]{:S(2)}) %copy-start.2) | copy-done | bytes 32
  3.2 55.7 %noise_correlation.1 = f32[2,64,512]{2,1,0:T(8,128)S(1)} custom-call(f32[8192,128]{1,0:T(8,128)} %bitcast.5, s32[1,2]{1,0:T(1,128)S(1)} %copy-done.2, bf16[7,2,128,1024]{3,2,1,0:T(8,128)(2,1)} %constant.6.clone.odd_ref, bf16[2,2,64,512]{3,2,1,0:T(8,128)(2,1)S(1)} %copy-done.1, bf16[1024,1024]{1,0:T(8,128)(2,1)S(1)} %copy-done), custom_call_target="tpu_custom_call" | custom-call | tf_op jit(solution)/shard_map/noise_correlation/pallas_call | solution.py:315
  58.9 0.7 %copy.8 = f32[2,1,64,512]{3,2,1,0:T(8,128)} copy(f32[2,1,64,512]{3,2,1,0:T(8,128)S(1)} %bitcast.4) | data formatting | bytes 524288
Async XLA Ops:
  0.0 1.6 %copy-start = (bf16[1024,1024]{1,0:T(8,128)(2,1)S(1)}, bf16[1024,1024]{1,0:T(8,128)(2,1)}, u32[]{:S(2)}) copy-start(bf16[1024,1024]{1,0:T(8,128)(2,1)} %constant.8.clone.lag_ref) | copy-start | bytes 6291460
  1.6 0.9 %copy-start.1 = (bf16[2,2,64,512]{3,2,1,0:T(8,128)(2,1)S(1)}, bf16[2,2,64,512]{3,2,1,0:T(8,128)(2,1)}, u32[]{:S(2)}) copy-start(bf16[2,2,64,512]{3,2,1,0:T(8,128)(2,1)} %constant.7.clone.even_ref) | copy-start | bytes 786436
  2.5 0.7 %copy-start.2 = (s32[1,2]{1,0:T(1,128)S(1)}, s32[1,2]{1,0:T(1,128)}, u32[]{:S(2)}) copy-start(s32[1,2]{1,0:T(1,128)} %pair_ref.1) | copy-start | bytes 28

commit v2 on v1

v2 whole, which is shorter than its diff:
```python
import functools
import math

import jax
import jax.numpy as jnp
import ml_dtypes
import numpy as np
from jax import lax
from jax.experimental import pallas as pl
from jax.experimental.pallas import tpu as pltpu
from jax.sharding import PartitionSpec as P

L = 8192
LAGS = 512
K0 = 256
BANDS = 512
STA = 8
WIN = 32
ST = 128
SEG = 64
RADIX = 16
FOLD = L // RADIX
MESH = pl.DeviceIdType.MESH


def bin_of():
    bins = np.zeros((WIN, STA, 2), np.int64)
    for z in range(STA):
        for q in range(1, 8):
            for u in range(4):
                m = 16 + 4 * z + u
                bins[4 * (q - 1) + u, z] = (16 * m + q, 16 * m + 16 - q)
        for half in range(2):
            for u in range(2):
                for s in range(2):
                    bins[28 + 2 * half + u, z, s] = 16 * (16 + 4 * z + 2 * u + s) + 8 * half
    return bins


def split(table):
    high = table.astype(ml_dtypes.bfloat16)
    low = (table - high.astype(np.float64)).astype(ml_dtypes.bfloat16)
    return high, low


@functools.cache
def tables():
    bins = bin_of()
    n = np.arange(FOLD)

    def trig(k):
        angle = 2 * math.pi * ((k * n) % L) / L
        return np.cos(angle), np.sin(angle)

    odd = np.zeros((7, 4, STA, 2, 2, 2 * FOLD))
    for q in range(1, 8):
        for u in range(4):
            for z in range(STA):
                for s in range(2):
                    c, d = trig(bins[4 * (q - 1) + u, z, s])
                    sign = 1.0 if s == 0 else -1.0
                    odd[q - 1, u, z, s, 0] = np.concatenate([c, sign * d])
                    odd[q - 1, u, z, s, 1] = np.concatenate([-d, sign * c])
    even = np.zeros((2, 2, STA, 2, 2, FOLD))
    for half in range(2):
        for u in range(2):
            for z in range(STA):
                for s in range(2):
                    c, d = trig(bins[28 + 2 * half + u, z, s])
                    even[half, u, z, s, 0] = c
                    even[half, u, z, s, 1] = -d
    shifts = (np.arange(LAGS) - LAGS // 2) % L
    angle = 2 * math.pi * ((bins[..., None] * shifts) % L) / L
    lag = np.stack([np.cos(angle), -np.sin(angle)], axis=3)
    lag = lag.transpose(2, 0, 1, 3, 4).reshape(2 * BANDS, LAGS).T * float(WIN * BANDS) ** (-0.5)
    odd = odd.transpose(0, 1, 3, 2, 4, 5).reshape(7, 128, 2 * FOLD)
    odd = np.stack(split(odd), axis=1)
    even = even.transpose(0, 1, 3, 2, 4, 5).reshape(2, 64, FOLD)
    even = np.stack(split(even), axis=1)
    lag = np.concatenate(split(lag), axis=0)
    return odd, even, lag


def fold16(x):
    r2 = math.sqrt(0.5)
    c1 = math.cos(math.pi / 8)
    c3 = math.sin(math.pi / 8)
    e = [x[a] + x[a + 8] for a in range(8)]
    o = [x[a] - x[a + 8] for a in range(8)]
    f = [e[a] + e[a + 4] for a in range(4)]
    g = [e[a] - e[a + 4] for a in range(4)]
    f02, f13 = f[0] + f[2], f[1] + f[3]
    gd, gs = r2 * (g[1] - g[3]), r2 * (g[1] + g[3])
    d = [None] + [o[a] - o[8 - a] for a in range(1, 4)]
    s = [None] + [o[a] + o[8 - a] for a in range(1, 4)]
    d2, s2 = r2 * d[2], r2 * s[2]
    p, m = o[0] + d2, o[0] - d2
    u, v = c1 * d[1] + c3 * d[3], c3 * d[1] - c1 * d[3]
    pp, mm = s2 + o[4], s2 - o[4]
    uu, vv = c3 * s[1] + c1 * s[3], c1 * s[1] - c3 * s[3]
    real = [f02 + f13, p + u, g[0] + gd, m + v, f[0] - f[2], m - v, g[0] - gd, p - u, f02 - f13]
    imag = [None, -(uu + pp), -(g[2] + gs), -(vv + mm), f[3] - f[1], mm - vv, g[2] - gs, pp - uu]
    return real, imag


def far_first_win():
    offsets = [(y, x, c) for y in range(4) for x in range(4) for c in range(2)][1:]
    return sorted(offsets, key=lambda o: -(10 * (min(o[0], 4 - o[0]) + min(o[1], 4 - o[1])) + o[2]))


FAR_FIRST_STA = (4, 3, 5, 2, 6, 1, 7)


def kernel(
    x_ref, pair_ref, odd_ref, even_ref, lag_ref, out_ref,
    x_v, odd_v, even_v, lag_v, pairs, fodd, feven, spec, rows, total, order,
    asend, arecv, bsend, brecv_0, brecv_1, csend, crecv, dsend, drecv,
    x_sem, t_sem, send_sem, p_sem, a_sem, b_sem, c_sem, d_sem,
):
    me_s = lax.axis_index("sta")
    me_w = lax.axis_index("win")
    y, x, core = me_w // 8, lax.rem(me_w // 2, 4), lax.rem(me_w, 2)
    ys = [lax.rem(y + d, 4) * 8 for d in range(4)]
    xs = [lax.rem(x + d, 4) * 2 for d in range(4)]
    cores = [core, 1 - core]
    win_peers = [ys[dy] + xs[dx] + cores[dc] for dy, dx, dc in far_first_win()]
    sta_peers = [lax.rem(me_s + d, STA) for d in FAR_FIRST_STA]

    x_copies = [
        pltpu.make_async_copy(x_ref.at[pl.ds(2048 * i, 2048)], x_v.at[pl.ds(2048 * i, 2048)], x_sem.at[i])
        for i in range(4)
    ]
    t_copies = [
        pltpu.make_async_copy(src, dst, t_sem.at[i])
        for i, (src, dst) in enumerate(((odd_ref, odd_v), (even_ref, even_v), (lag_ref, lag_v)))
    ]

    brecv = (brecv_0, brecv_1)
    barrier = pltpu.get_barrier_semaphore()
    for peer in win_peers:
        pl.semaphore_signal(barrier, inc=1, device_id={"win": peer}, device_id_type=MESH)
    for peer in sta_peers:
        pl.semaphore_signal(barrier, inc=1, device_id={"sta": peer}, device_id_type=MESH)
    for copy in x_copies + t_copies:
        copy.start()

    def send(src, dst, phase, recv_sem, axis, peer):
        pltpu.make_async_remote_copy(
            src_ref=src, dst_ref=dst, send_sem=send_sem.at[phase], recv_sem=recv_sem,
            device_id={axis: peer}, device_id_type=MESH,
        ).start()

    def wait(ref, sem):
        pltpu.make_async_copy(ref, ref, sem).wait()

    for chunk in range(4):
        x_copies[chunk].wait()

        def fold(t, _, chunk=chunk):
            lane_tile = lax.rem(t, 4)
            i2 = t // 4
            first = chunk * 2048 + i2 * 64
            x = [x_v[pl.ds(first + 4 * a + lane_tile, 16, stride=128), :] for a in range(RADIX)]
            real, imag = fold16(x)
            row = pl.multiple_of((chunk // 2) * 64 + i2 * 32 + (chunk % 2) * 16, 16)
            lane = pl.multiple_of(lane_tile * 128, 128)

            def put(dst, at, value):
                high = value.astype(jnp.bfloat16)
                low = (value - high.astype(jnp.float32)).astype(jnp.bfloat16)
                dst[pl.ds(row, 16), pl.ds(at, 128)] = high
                dst[pl.ds(row + 128, 16), pl.ds(at, 128)] = low

            put(feven.at[0], lane, real[0])
            put(feven.at[1], lane, real[8])
            for q in range(1, 8):
                put(fodd.at[q - 1], lane, real[q])
                put(fodd.at[q - 1], pl.multiple_of(lane + FOLD, 128), imag[q])
            return 0

        lax.fori_loop(0, 8, fold, 0)

    contract_last = (((1,), (1,)), ((), ()))

    def dft(table, data):
        high = lax.dot_general(table[0], data, contract_last, preferred_element_type=jnp.float32)
        low = lax.dot_general(table[1], data[:ST], contract_last, preferred_element_type=jnp.float32)
        return high[:, :ST] + (high[:, ST:] + low)

    t_copies[0].wait()

    def odd_class(q, power):
        value = dft(odd_v[q], fodd[q])
        spec[pl.ds(pl.multiple_of(q * 128, 128), 128), :] = value
        return power + jnp.sum((value * value).reshape(16, 8, ST), axis=0)

    power = lax.fori_loop(0, 7, odd_class, jnp.zeros((8, ST), jnp.float32))
    t_copies[1].wait()
    for half in range(2):
        value = dft(even_v[half], feven[half])
        spec[896 + 64 * half : 960 + 64 * half, :] = value
        power = power + jnp.sum((value * value).reshape(8, 8, ST), axis=0)
    mean = jnp.sum(power, axis=0, keepdims=True) * (1.0 / BANDS)
    inverse = 1.0 / jnp.sqrt(mean + 1e-06)
    for w in range(WIN):
        asend[w] = (spec[32 * w : 32 * w + 32, :] * inverse).astype(jnp.bfloat16).reshape(2, 16, ST)

    pl.semaphore_wait(barrier, STA - 1 + WIN - 1)

    for s in range(2):
        for peer in win_peers:
            send(asend.at[peer, s], arecv.at[s, me_w], 0, a_sem.at[s], "win", peer)
        arecv[s, me_w] = asend[me_w, s]
    for peer in sta_peers:
        send(pair_ref, pairs.at[me_s], 4, p_sem, "sta", peer)
    pairs[me_s, 0, 0] = pair_ref[0, 0]
    pairs[me_s, 0, 1] = pair_ref[0, 1]

    for s in range(2):
        wait(arecv.at[s, pl.ds(0, WIN - 1)], a_sem.at[s])
        rows[...] = arecv[s].reshape(WIN * 16, ST).astype(jnp.float32)
        for column in sta_peers + [me_s]:
            for c in range(2):
                part = rows[pl.ds(2 * column + c, WIN, stride=16), :].astype(jnp.bfloat16)
                bsend[column, s, WIN * c : WIN * c + WIN, :] = part
            if column is not me_s:
                send(bsend.at[column, s], brecv[s].at[me_s], 1, b_sem.at[s], "sta", column)
        brecv[s][me_s] = bsend[me_s, s]

    left_lanes = lax.broadcasted_iota(jnp.int32, (WIN, ST), 1) < 64

    def cross(p, s):
        a = pairs[p, 0, 0]
        b = pairs[p, 0, 1]
        a_odd = lax.rem(a, 2) == 1
        b_odd = lax.rem(b, 2) == 1
        left = brecv[s][a // 2]
        second = brecv[s][b // 2].astype(jnp.float32)
        re, im = second[:WIN], second[WIN:]
        re_roll, im_roll = pltpu.roll(re, 64, 1), pltpu.roll(im, 64, 1)
        re_l, im_l = jnp.where(b_odd, re_roll, re), jnp.where(b_odd, im_roll, im)
        re_r, im_r = jnp.where(b_odd, re, re_roll), jnp.where(b_odd, im, im_roll)
        right = jnp.concatenate(
            [jnp.where(left_lanes, re_l, -im_r), jnp.where(left_lanes, im_l, re_r)], axis=0
        ).astype(jnp.bfloat16)
        prod = lax.dot_general(left, right, (((0,), (0,)), ((), ())), preferred_element_type=jnp.float32)
        prod = jnp.where(a_odd, prod[64:], prod[:64])
        top, low = prod[:32], prod[32:]
        value = jnp.concatenate(
            [jnp.where(left_lanes, top, pltpu.roll(low, 64, 1)), jnp.where(left_lanes, pltpu.roll(top, 64, 1), low)],
            axis=0,
        ).reshape(8, 8, ST)
        largest = jnp.maximum(jnp.max(jnp.abs(value), axis=0), 1e-30)
        exponent = jnp.floor(jnp.log(largest) * (1.0 / math.log(2.0))) + 1.0
        scaled = jnp.round(value * jnp.exp2(15.0 - exponent)[None])
        scaled = jnp.clip(scaled, -32767.0, 32767.0).reshape(64, ST)
        csend[p, s, :64, :] = scaled.astype(jnp.int32).astype(jnp.int16)
        csend[p, s, 64:, :] = jnp.concatenate([exponent, exponent], axis=0).astype(jnp.int32).astype(jnp.int16)

    for s in range(2):
        wait(brecv[s].at[pl.ds(0, STA - 1)], b_sem.at[s])
        if s == 0:
            wait(pairs.at[pl.ds(0, STA - 1)], p_sem)
        for p in sta_peers:
            cross(p, s)
            send(csend.at[p, s], crecv.at[me_s, s], 2, c_sem.at[s], "sta", p)
        cross(me_s, s)
        crecv[me_s, s] = csend[me_s, s]

    for s in range(2):
        wait(crecv.at[pl.ds(0, STA - 1), s], c_sem.at[s])
        for z in range(STA):
            scale = jnp.exp2(crecv[z, s, 64:, :].astype(jnp.float32)[:8] - 15.0)
            value = crecv[z, s, :64, :].astype(jnp.float32).reshape(8, 8, ST) * scale[None]
            rows[64 * z : 64 * z + 64, :] = value.reshape(64, ST)
        for w in win_peers + [me_w]:
            dsend[w, s] = rows[pl.ds(w, 16, stride=32), :]
            if w is not me_w:
                send(dsend.at[w, s], drecv.at[s, me_w], 3, d_sem.at[s], "win", w)
        drecv[s, me_w] = dsend[me_w, s]

    t_copies[2].wait()
    wait(asend.at[pl.ds(0, WIN - 1)], send_sem.at[0])
    wait(bsend.at[pl.ds(0, STA - 1)], send_sem.at[1])
    wait(csend.at[pl.ds(0, STA - 1)], send_sem.at[2])
    wait(pairs.at[pl.ds(0, STA - 1)], send_sem.at[4])

    for s in range(2):
        wait(drecv.at[s, pl.ds(0, WIN - 1)], d_sem.at[s])
        value = drecv[s].reshape(BANDS, ST)
        high = value.astype(jnp.bfloat16)
        low = (value - high.astype(jnp.float32)).astype(jnp.bfloat16)
        both = jnp.concatenate([high, low], axis=1)

        def lags(t, _, s=s, both=both, high=high):
            row = pl.multiple_of(t * 128, 128)
            lane = pl.multiple_of(s * BANDS, 128)
            value = jnp.dot(
                lag_v[pl.ds(row, 128), pl.ds(lane, BANDS)], both, preferred_element_type=jnp.float32
            )
            extra = jnp.dot(
                lag_v[pl.ds(row + LAGS, 128), pl.ds(lane, BANDS)], high, preferred_element_type=jnp.float32
            )
            value = value[:, :ST] + (value[:, ST:] + extra)
            if s == 0:
                total[pl.ds(row, 128), :] = value
                return 0
            value = jnp.transpose(value + total[pl.ds(row, 128), :])
            for i2 in range(2):
                for j2 in range(2):
                    part = value[(2 * i2 + j2) * 32 : (2 * i2 + j2) * 32 + 32]
                    order[pl.ds(i2 * 64 + j2, 32, stride=2), :] = part
            out_ref[:, :, pl.ds(row, 128)] = order[...].reshape(2, 64, 128)
            return 0

        lax.fori_loop(0, LAGS // 128, lags, 0)
    wait(dsend.at[pl.ds(0, WIN - 1)], send_sem.at[3])


def body(traces, pair_blocks):
    odd, even, lag = (jnp.asarray(t) for t in tables())
    f32, bf16, i16 = jnp.float32, jnp.bfloat16, jnp.int16
    hbm = pl.BlockSpec(memory_space=pltpu.HBM)
    out = pl.pallas_call(
        kernel,
        out_shape=jax.ShapeDtypeStruct((2, 64, LAGS), f32),
        in_specs=[hbm, pl.BlockSpec(memory_space=pltpu.SMEM), hbm, hbm, hbm],
        out_specs=pl.BlockSpec(memory_space=pltpu.VMEM),
        scratch_shapes=[
            pltpu.VMEM((ST * SEG, 128), f32),
            pltpu.VMEM(odd.shape, bf16),
            pltpu.VMEM(even.shape, bf16),
            pltpu.VMEM(lag.shape, bf16),
            pltpu.SMEM((STA, 1, 2), jnp.int32),
            pltpu.VMEM((7, 2 * ST, 2 * FOLD), bf16),
            pltpu.VMEM((2, 2 * ST, FOLD), bf16),
            pltpu.VMEM((2 * BANDS, ST), f32),
            pltpu.VMEM((BANDS, ST), f32),
            pltpu.VMEM((LAGS, ST), f32),
            pltpu.VMEM((ST, 128), f32),
            pltpu.VMEM((WIN, 2, 16, ST), bf16),
            pltpu.VMEM((2, WIN, 16, ST), bf16),
            pltpu.VMEM((STA, 2, 2 * WIN, ST), bf16),
            pltpu.VMEM((STA, 2 * WIN, ST), bf16),
            pltpu.VMEM((STA, 2 * WIN, ST), bf16),
            pltpu.VMEM((STA, 2, 80, ST), i16),
            pltpu.VMEM((STA, 2, 80, ST), i16),
            pltpu.VMEM((WIN, 2, 16, ST), f32),
            pltpu.VMEM((2, WIN, 16, ST), f32),
            pltpu.SemaphoreType.DMA((4,)),
            pltpu.SemaphoreType.DMA((3,)),
            pltpu.SemaphoreType.DMA((5,)),
            pltpu.SemaphoreType.DMA,
            pltpu.SemaphoreType.DMA((2,)),
            pltpu.SemaphoreType.DMA((2,)),
            pltpu.SemaphoreType.DMA((2,)),
            pltpu.SemaphoreType.DMA((2,)),
        ],
        compiler_params=pltpu.CompilerParams(
            collective_id=0, has_side_effects=True, vmem_limit_bytes=48 * 1024 * 1024
        ),
        name="noise_correlation",
    )(traces.reshape(ST * SEG, 128), pair_blocks, odd, even, lag)
    return out.reshape(2, 1, 64, LAGS)


def solution(mesh):
    in_specs = (P("sta", "win", None), P("sta", None))
    out_specs = P("win", "sta", None, None)
    return jax.shard_map(body, mesh=mesh, in_specs=in_specs, out_specs=out_specs, check_vma=False)
```

time: 59.7 us -> 47.2 us (0.79)
  Pallas kernels: 55.7 us -> 43.1 us
    pallas_call x1, Pallas kernels: 55.7 us -> 43.1 us  [body(): pl.pallas_call(kernel, out_shape=jax.ShapeDtypeStruct((2, 64, LAGS), f32)...]
where the time goes in v2:
time: 47.2 us; the launch traced here: 47.1 us
  Pallas kernels  43.1 us (91%)
  local copies, waits for them, and re-layouts  3.9 us (8%)
    pallas_call x1, Pallas kernels, body(): pl.pallas_call(kernel, out_shape=jax.ShapeDtypeStruct((2, 64, LAGS), f32)...  43.1 us
    unnamed x7, local copies, waits for them, and re-layouts  3.9 us

profile of v2, /device:TPU:1, one launch (start us, length us, event | category | flops | bytes accessed | tf_op | source)
XLA Modules:
  0.0 47.1 jit_solution(7861780795765801763)
XLA Ops:
  0.0 0.0 copy-start
  0.0 1.6 %copy-done = bf16[1024,1024]{1,0:T(8,128)(2,1)S(1)} copy-done((bf16[1024,1024]{1,0:T(8,128)(2,1)S(1)}, bf16[1024,1024]{1,0:T(8,128)(2,1)}, u32[]{:S(2)}) %copy-start) | copy-done | bytes 2097176
  1.6 0.0 copy-start.1
  1.6 0.9 %copy-done.1 = bf16[2,2,64,512]{3,2,1,0:T(8,128)(2,1)S(1)} copy-done((bf16[2,2,64,512]{3,2,1,0:T(8,128)(2,1)S(1)}, bf16[2,2,64,512]{3,2,1,0:T(8,128)(2,1)}, u32[]{:S(2)}) %copy-start.1) | copy-done | bytes 262168
  2.5 0.0 copy-start.2
  2.5 0.7 %copy-done.2 = s32[1,2]{1,0:T(1,128)S(1)} copy-done((s32[1,2]{1,0:T(1,128)S(1)}, s32[1,2]{1,0:T(1,128)}, u32[]{:S(2)}) %copy-start.2) | copy-done | bytes 32
  3.2 43.1 %noise_correlation.1 = f32[2,64,512]{2,1,0:T(8,128)S(1)} custom-call(f32[8192,128]{1,0:T(8,128)} %bitcast.5, s32[1,2]{1,0:T(1,128)S(1)} %copy-done.2, bf16[7,2,128,1024]{3,2,1,0:T(8,128)(2,1)} %constant.6.clone.odd_ref, bf16[2,2,64,512]{3,2,1,0:T(8,128)(2,1)S(1)} %copy-done.1, bf16[1024,1024]{1,0:T(8,128)(2,1)S(1)} %copy-done), custom_call_target="tpu_custom_call" | custom-call | tf_op jit(solution)/shard_map/noise_correlation/pallas_call | solution.py:324
  46.4 0.7 %copy.8 = f32[2,1,64,512]{3,2,1,0:T(8,128)} copy(f32[2,1,64,512]{3,2,1,0:T(8,128)S(1)} %bitcast.4) | data formatting | bytes 524288
Async XLA Ops:
  0.0 1.6 %copy-start = (bf16[1024,1024]{1,0:T(8,128)(2,1)S(1)}, bf16[1024,1024]{1,0:T(8,128)(2,1)}, u32[]{:S(2)}) copy-start(bf16[1024,1024]{1,0:T(8,128)(2,1)} %constant.8.clone.lag_ref) | copy-start | bytes 6291460
  1.6 0.9 %copy-start.1 = (bf16[2,2,64,512]{3,2,1,0:T(8,128)(2,1)S(1)}, bf16[2,2,64,512]{3,2,1,0:T(8,128)(2,1)}, u32[]{:S(2)}) copy-start(bf16[2,2,64,512]{3,2,1,0:T(8,128)(2,1)} %constant.7.clone.even_ref) | copy-start | bytes 786436
  2.5 0.7 %copy-start.2 = (s32[1,2]{1,0:T(1,128)S(1)}, s32[1,2]{1,0:T(1,128)}, u32[]{:S(2)}) copy-start(s32[1,2]{1,0:T(1,128)} %pair_ref.1) | copy-start | bytes 28

commit v3 on v1

--- a/solution.py
+++ b/solution.py
@@ -72,7 +72,7 @@
     shifts = (np.arange(LAGS) - LAGS // 2) % L
     angle = 2 * math.pi * ((bins[..., None] * shifts) % L) / L
     lag = np.stack([np.cos(angle), -np.sin(angle)], axis=3)
-    lag = lag.reshape(2 * BANDS, LAGS).T * float(WIN * BANDS) ** (-0.5)
+    lag = lag.transpose(2, 3, 1, 0, 4).reshape(2 * BANDS, LAGS).T * float(WIN * BANDS) ** (-0.5)
     odd = np.stack(split(odd.reshape(7, 128, 2 * FOLD)), axis=1)
     even = np.stack(split(even.reshape(2, 64, FOLD)), axis=1)
     lag = np.concatenate(split(lag), axis=0)
@@ -101,14 +101,19 @@
     return real, imag
 
 
+FAR_FIRST = ((4,), (3, 5), (2, 6), (1, 7), (0,))
+ALL = STA * WIN
+
+
 def kernel(
     x_ref, pair_ref, odd_ref, even_ref, lag_ref, out_ref,
-    x_v, odd_v, even_v, lag_v, pairs, fodd, feven, spec,
-    asend, arecv, bsend, brecv, csend, crecv, dsend, drecv, order,
-    x_sem, t_sem, p_ssem, p_rsem, a_ssem, a_rsem, b_ssem, b_rsem, c_ssem, c_rsem, d_ssem, d_rsem,
+    x_v, odd_v, even_v, lag_v, pairs, fodd, feven, spec, rows, codes, order,
+    asend, arecv, bands, csend, crecv,
+    x_sem, t_sem, send_sem, p_sem, a_sem, c_sem,
 ):
     me_s = lax.axis_index("sta")
     me_w = lax.axis_index("win")
+    me = me_s * WIN + me_w
 
     x_copies = [
         pltpu.make_async_copy(x_ref.at[pl.ds(2048 * i, 2048)], x_v.at[pl.ds(2048 * i, 2048)], x_sem.at[i])
@@ -121,18 +126,37 @@
     for copy in x_copies + t_copies:
         copy.start()
 
+    def column(offset):
+        return lax.rem(me_s + offset, STA)
+
+    def to_others(action):
+        def in_columns(offsets):
+            def step(i, _):
+                w = lax.rem(me_w + (1 if 0 in offsets else 20) + i, WIN)
+                for offset in offsets:
+                    action(column(offset), w)
+                return 0
+
+            lax.fori_loop(0, WIN - 1 if 0 in offsets else WIN, step, 0)
+
+        for offsets in FAR_FIRST:
+            in_columns(offsets)
+
     barrier = pltpu.get_barrier_semaphore()
 
-    def greet(axis, me, count):
-        def step(i, _):
-            peer = lax.rem(me + i, count)
-            pl.semaphore_signal(barrier, inc=1, device_id={axis: peer}, device_id_type=MESH)
-            return 0
-
-        lax.fori_loop(1, count, step, 0)
-
-    greet("sta", me_s, STA)
-    greet("win", me_w, WIN)
+    def greet(z, w):
+        pl.semaphore_signal(barrier, inc=1, device_id={"sta": z, "win": w}, device_id_type=MESH)
+
+    to_others(greet)
+
+    def send(src, dst, phase, recv_sem, z, w):
+        pltpu.make_async_remote_copy(
+            src_ref=src, dst_ref=dst, send_sem=send_sem.at[phase], recv_sem=recv_sem,
+            device_id={"sta": z, "win": w}, device_id_type=MESH,
+        ).start()
+
+    def wait(ref, sem):
+        pltpu.make_async_copy(ref, ref, sem).wait()
 
     for chunk in range(4):
         x_copies[chunk].wait()
@@ -183,108 +207,93 @@
         power = power + jnp.sum((value * value).reshape(8, 8, ST), axis=0)
     mean = jnp.sum(power, axis=0, keepdims=True) * (1.0 / BANDS)
     inverse = 1.0 / jnp.sqrt(mean + 1e-06)
-    for i in range(WIN):
-        asend[i] = (spec[32 * i : 32 * i + 32, :] * inverse).astype(jnp.bfloat16)
-
-    pl.semaphore_wait(barrier, STA - 1 + WIN - 1)
-
-    def p_copy(peer, slot):
-        return pltpu.make_async_remote_copy(
-            src_ref=pair_ref, dst_ref=pairs.at[slot], send_sem=p_ssem.at[peer], recv_sem=p_rsem.at[slot],
-            device_id={"sta": peer}, device_id_type=MESH,
-        )
-
-    def a_copy(peer, slot):
-        return pltpu.make_async_remote_copy(
-            src_ref=asend.at[peer], dst_ref=arecv.at[slot], send_sem=a_ssem.at[peer], recv_sem=a_rsem.at[slot],
-            device_id={"win": peer}, device_id_type=MESH,
-        )
-
-    def b_copy(peer, slot):
-        return pltpu.make_async_remote_copy(
-            src_ref=bsend.at[peer], dst_ref=brecv.at[slot], send_sem=b_ssem.at[peer], recv_sem=b_rsem.at[slot],
-            device_id={"sta": peer}, device_id_type=MESH,
-        )
-
-    def c_copy(peer, slot):
-        return pltpu.make_async_remote_copy(
-            src_ref=csend.at[peer], dst_ref=crecv.at[slot], send_sem=c_ssem.at[peer], recv_sem=c_rsem.at[slot],
-            device_id={"sta": peer}, device_id_type=MESH,
-        )
-
-    def d_copy(peer, slot):
-        return pltpu.make_async_remote_copy(
-            src_ref=dsend.at[peer], dst_ref=drecv.at[slot], send_sem=d_ssem.at[peer], recv_sem=d_rsem.at[slot],
-            device_id={"win": peer}, device_id_type=MESH,
-        )
-
-    def each(count, me, action):
-        def step(i, _):
-            action(lax.rem(me + i, count))
-            return 0
-
-        lax.fori_loop(1, count, step, 0)
-
-    each(WIN, me_w, lambda peer: a_copy(peer, me_w).start())
-    each(STA, me_s, lambda peer: p_copy(peer, me_s).start())
-    arecv[me_w] = asend[me_w]
+    for i in range(ALL // 8):
+        white = (spec[32 * i : 32 * i + 32, :] * inverse).astype(jnp.bfloat16)
+        asend[8 * i : 8 * i + 8] = white.reshape(8, 4, ST)
+
+    pl.semaphore_wait(barrier, ALL - 1)
+
+    to_others(lambda z, w: send(asend.at[w * STA + z], arecv.at[me], 0, a_sem, z, w))
+    for offsets in FAR_FIRST[:-1]:
+        for offset in offsets:
+            send(pair_ref, pairs.at[me_s], 2, p_sem, column(offset), me_w)
+    arecv[me] = asend[me_w * STA + me_s]
     pairs[me_s, 0, 0] = pair_ref[0, 0]
     pairs[me_s, 0, 1] = pair_ref[0, 1]
-    each(WIN, me_w, lambda peer: a_copy(peer, peer).wait_recv())
+    wait(arecv.at[pl.ds(0, ALL - 1)], a_sem)
 
     for z in range(STA):
-        bsend[z] = jnp.swapaxes(arecv[:, 4 * z : 4 * z + 4, :], 0, 1)
-    each(STA, me_s, lambda peer: b_copy(peer, me_s).start())
-    brecv[me_s] = bsend[me_s]
-    each(STA, me_s, lambda peer: b_copy(peer, peer).wait_recv())
-    each(STA, me_s, lambda peer: p_copy(peer, peer).wait_recv())
+        part = arecv[WIN * z : WIN * z + WIN].astype(jnp.float32)
+        rows[128 * z : 128 * z + 128, :] = part.reshape(4 * WIN, ST)
+    for z in range(STA):
+        for r in range(4):
+            part = rows[pl.ds(128 * z + r, WIN, stride=4), :]
+            bands[z, WIN * r : WIN * r + WIN, :] = part.astype(jnp.bfloat16)
+    wait(pairs.at[pl.ds(0, STA - 1)], p_sem)
 
     left_lanes = lax.broadcasted_iota(jnp.int32, (WIN, ST), 1) < 64
 
-    def one_pair(i, _):
-        p = lax.rem(me_s + i, STA)
+    def cross(p):
         a = pairs[p, 0, 0]
         b = pairs[p, 0, 1]
         a_odd = lax.rem(a, 2) == 1
         b_odd = lax.rem(b, 2) == 1
-        first = brecv[a // 2]
-        second = brecv[b // 2].astype(jnp.float32)
+        first = bands[a // 2]
+        second = bands[b // 2].astype(jnp.float32)
+        parts = []
         for s in range(2):
-            re, im = second[2 * s], second[2 * s + 1]
+            re, im = second[64 * s : 64 * s + 32], second[64 * s + 32 : 64 * s + 64]
             re_roll, im_roll = pltpu.roll(re, 64, 1), pltpu.roll(im, 64, 1)
             re_l, im_l = jnp.where(b_odd, re_roll, re), jnp.where(b_odd, im_roll, im)
             re_r, im_r = jnp.where(b_odd, re, re_roll), jnp.where(b_odd, im, im_roll)
             right = jnp.concatenate(
                 [jnp.where(left_lanes, re_l, -im_r), jnp.where(left_lanes, im_l, re_r)], axis=0
             ).astype(jnp.bfloat16)
-            left = first[2 * s : 2 * s + 2].reshape(2 * WIN, ST)
+            left = first[64 * s : 64 * s + 64]
             prod = lax.dot_general(left, right, (((0,), (0,)), ((), ())), preferred_element_type=jnp.float32)
             prod = jnp.where(a_odd, prod[64:], prod[:64])
             top, low = prod[:32], prod[32:]
-            csend[p, 64 * s : 64 * s + 32, :] = jnp.where(left_lanes, top, pltpu.roll(low, 64, 1))
-            csend[p, 64 * s + 32 : 64 * s + 64, :] = jnp.where(left_lanes, pltpu.roll(top, 64, 1), low)
-
-        @pl.when(i < STA)
-        def _():
-            c_copy(p, me_s).start()
-
-        return 0
-
-    lax.fori_loop(1, STA + 1, one_pair, 0)
-    crecv[me_s] = csend[me_s]
-    each(STA, me_s, lambda peer: c_copy(peer, peer).wait_recv())
-
-    for w in range(WIN):
-        for z in range(STA):
-            dsend[w, 4 * z : 4 * z + 4, :] = crecv[z, pl.ds(w, 4, stride=32), :]
-    each(WIN, me_w, lambda peer: d_copy(peer, me_w).start())
-    drecv[me_w] = dsend[me_w]
+            parts.append(jnp.where(left_lanes, top, pltpu.roll(low, 64, 1)))
+            parts.append(jnp.where(left_lanes, pltpu.roll(top, 64, 1), low))
+        return parts
+
+    def encode(p, parts):
+        largest = functools.reduce(jnp.maximum, [jnp.abs(v) for v in parts])
+        exponent = jnp.floor(jnp.log(jnp.maximum(largest, 1e-30)) * (1.0 / math.log(2.0))) + 1.0
+        scale = jnp.exp2(13.0 - exponent)
+        exponent = exponent.astype(jnp.int32) + 128
+        for r, v in enumerate(parts):
+            value = jnp.clip(jnp.round(v * scale), -8191.0, 8191.0).astype(jnp.int32)
+            codes[pl.ds(r, WIN, stride=4), :] = value * 4 + (jnp.right_shift(exponent, 2 * r) & 3)
+        csend[pl.ds(WIN * p, WIN)] = codes[:128, :].astype(jnp.int16).reshape(WIN, 4, ST)
+
+    for offsets in FAR_FIRST:
+        for offset in offsets:
+            p = column(offset)
+            encode(p, cross(p))
+
+            def step(i, _, p=p, offset=offset):
+                w = lax.rem(me_w + (20 if offset else 1) + i, WIN)
+                send(csend.at[p * WIN + w], crecv.at[me], 1, c_sem, p, w)
+                return 0
+
+            lax.fori_loop(0, WIN if offset else WIN - 1, step, 0)
+    crecv[me] = csend[me]
+
     t_copies[2].wait()
-    each(WIN, me_w, lambda peer: d_copy(peer, peer).wait_recv())
-
-    cross = drecv[...].reshape(WIN * 32, ST)
-    high = cross.astype(jnp.bfloat16)
-    low = (cross - high.astype(jnp.float32)).astype(jnp.bfloat16)
+    wait(asend.at[pl.ds(0, ALL - 1)], send_sem.at[0])
+    wait(pairs.at[pl.ds(0, STA - 1)], send_sem.at[2])
+    wait(crecv.at[pl.ds(0, ALL - 1)], c_sem)
+
+    for z in range(STA):
+        part = crecv[WIN * z : WIN * z + WIN].astype(jnp.int32)
+        codes[128 * z : 128 * z + 128, :] = part.reshape(4 * WIN, ST)
+    coded = [codes[pl.ds(r, ALL, stride=4), :] for r in range(4)]
+    exponent = functools.reduce(jnp.bitwise_or, [jnp.left_shift(v & 3, 2 * r) for r, v in enumerate(coded)])
+    scale = jnp.exp2((exponent - 141).astype(jnp.float32))
+    value = jnp.concatenate([jnp.right_shift(v, 2).astype(jnp.float32) * scale for v in coded], axis=0)
+    high = value.astype(jnp.bfloat16)
+    low = (value - high.astype(jnp.float32)).astype(jnp.bfloat16)
     both = jnp.concatenate([high, low], axis=1)
 
     def lags(t, _):
@@ -300,18 +309,13 @@
         return 0
 
     lax.fori_loop(0, LAGS // 128, lags, 0)
-
-    each(WIN, me_w, lambda peer: a_copy(peer, me_w).wait_send())
-    each(STA, me_s, lambda peer: p_copy(peer, me_s).wait_send())
-    each(STA, me_s, lambda peer: b_copy(peer, me_s).wait_send())
-    each(STA, me_s, lambda peer: c_copy(peer, me_s).wait_send())
-    each(WIN, me_w, lambda peer: d_copy(peer, me_w).wait_send())
+    wait(csend.at[pl.ds(0, ALL - 1)], send_sem.at[1])
 
 
 def body(traces, pair_blocks):
     odd, even, lag = (jnp.asarray(t) for t in tables())
-    f32, bf16 = jnp.float32, jnp.bfloat16
-    hbm = pl.BlockSpec(memory_space=pl.ANY)
+    f32, bf16, i16 = jnp.float32, jnp.bfloat16, jnp.int16
+    hbm = pl.BlockSpec(memory_space=pltpu.HBM)
     out = pl.pallas_call(
         kernel,
         out_shape=jax.ShapeDtypeStruct((2, 64, LAGS), f32),
@@ -326,19 +330,21 @@
             pltpu.VMEM((7, 2 * ST, 2 * FOLD), bf16),
             pltpu.VMEM((2, 2 * ST, FOLD), bf16),
             pltpu.VMEM((2 * BANDS, ST), f32),
-            pltpu.VMEM((WIN, 32, ST), bf16),
-            pltpu.VMEM((WIN, 32, ST), bf16),
-            pltpu.VMEM((STA, 4, WIN, ST), bf16),
-            pltpu.VMEM((STA, 4, WIN, ST), bf16),
-            pltpu.VMEM((STA, 128, ST), f32),
-            pltpu.VMEM((STA, 128, ST), f32),
-            pltpu.VMEM((WIN, 32, ST), f32),
-            pltpu.VMEM((WIN, 32, ST), f32),
+            pltpu.VMEM((2 * BANDS, ST), f32),
+            pltpu.VMEM((2 * BANDS, ST), jnp.int32),
             pltpu.VMEM((ST, 128), f32),
+            pltpu.VMEM((ALL, 4, ST), bf16),
+            pltpu.VMEM((ALL, 4, ST), bf16),
+            pltpu.VMEM((STA, 4 * WIN, ST), bf16),
+            pltpu.VMEM((ALL, 4, ST), i16),
+            pltpu.VMEM((ALL, 4, ST), i16),
             pltpu.SemaphoreType.DMA((4,)),
             pltpu.SemaphoreType.DMA((3,)),
-        ]
-        + [pltpu.SemaphoreType.DMA((n,)) for n in (STA, STA, WIN, WIN, STA, STA, STA, STA, WIN, WIN)],
+            pltpu.SemaphoreType.DMA((3,)),
+            pltpu.SemaphoreType.DMA,
+            pltpu.SemaphoreType.DMA,
+            pltpu.SemaphoreType.DMA,
+        ],
         compiler_params=pltpu.CompilerParams(
             collective_id=0, has_side_effects=True, vmem_limit_bytes=48 * 1024 * 1024
         ),

time: 59.7 us -> 44.5 us (0.75)
  Pallas kernels: 55.7 us -> 40.5 us
    pallas_call x1, Pallas kernels: 55.7 us -> 40.5 us  [body(): pl.pallas_call(kernel, out_shape=jax.ShapeDtypeStruct((2, 64, LAGS), f32)...]
where the time goes in v3:
time: 44.5 us; the launch traced here: 44.4 us
  Pallas kernels  40.5 us (91%)
  local copies, waits for them, and re-layouts  3.9 us (9%)
    pallas_call x1, Pallas kernels, body(): pl.pallas_call(kernel, out_shape=jax.ShapeDtypeStruct((2, 64, LAGS), f32)...  40.5 us
    unnamed x7, local copies, waits for them, and re-layouts  3.9 us

profile of v3, /device:TPU:1, one launch (start us, length us, event | category | flops | bytes accessed | tf_op | source)
XLA Modules:
  0.0 44.4 jit_solution(5650366216067933720)
XLA Ops:
  0.0 0.0 copy-start
  0.0 1.6 %copy-done = bf16[1024,1024]{1,0:T(8,128)(2,1)S(1)} copy-done((bf16[1024,1024]{1,0:T(8,128)(2,1)S(1)}, bf16[1024,1024]{1,0:T(8,128)(2,1)}, u32[]{:S(2)}) %copy-start) | copy-done | bytes 2097176
  1.6 0.0 copy-start.1
  1.6 0.9 %copy-done.1 = bf16[2,2,64,512]{3,2,1,0:T(8,128)(2,1)S(1)} copy-done((bf16[2,2,64,512]{3,2,1,0:T(8,128)(2,1)S(1)}, bf16[2,2,64,512]{3,2,1,0:T(8,128)(2,1)}, u32[]{:S(2)}) %copy-start.1) | copy-done | bytes 262168
  2.5 0.0 copy-start.2
  2.5 0.7 %copy-done.2 = s32[1,2]{1,0:T(1,128)S(1)} copy-done((s32[1,2]{1,0:T(1,128)S(1)}, s32[1,2]{1,0:T(1,128)}, u32[]{:S(2)}) %copy-start.2) | copy-done | bytes 32
  3.2 40.5 %noise_correlation.1 = f32[2,64,512]{2,1,0:T(8,128)S(1)} custom-call(f32[8192,128]{1,0:T(8,128)} %bitcast.5, s32[1,2]{1,0:T(1,128)S(1)} %copy-done.2, bf16[7,2,128,1024]{3,2,1,0:T(8,128)(2,1)} %constant.6.clone.odd_ref, bf16[2,2,64,512]{3,2,1,0:T(8,128)(2,1)S(1)} %copy-done.1, bf16[1024,1024]{1,0:T(8,128)(2,1)S(1)} %copy-done), custom_call_target="tpu_custom_call" | custom-call | tf_op jit(solution)/shard_map/noise_correlation/pallas_call | solution.py:319
  43.7 0.7 %copy.8 = f32[2,1,64,512]{3,2,1,0:T(8,128)} copy(f32[2,1,64,512]{3,2,1,0:T(8,128)S(1)} %bitcast.4) | data formatting | bytes 524288
Async XLA Ops:
  0.0 1.6 %copy-start = (bf16[1024,1024]{1,0:T(8,128)(2,1)S(1)}, bf16[1024,1024]{1,0:T(8,128)(2,1)}, u32[]{:S(2)}) copy-start(bf16[1024,1024]{1,0:T(8,128)(2,1)} %constant.8.clone.lag_ref) | copy-start | bytes 6291460
  1.6 0.9 %copy-start.1 = (bf16[2,2,64,512]{3,2,1,0:T(8,128)(2,1)S(1)}, bf16[2,2,64,512]{3,2,1,0:T(8,128)(2,1)}, u32[]{:S(2)}) copy-start(bf16[2,2,64,512]{3,2,1,0:T(8,128)(2,1)} %constant.7.clone.even_ref) | copy-start | bytes 786436
  2.5 0.7 %copy-start.2 = (s32[1,2]{1,0:T(1,128)S(1)}, s32[1,2]{1,0:T(1,128)}, u32[]{:S(2)}) copy-start(s32[1,2]{1,0:T(1,128)} %pair_ref.1) | copy-start | bytes 28

commit v4 on v3

--- a/solution.py
+++ b/solution.py
@@ -20,6 +20,7 @@
 SEG = 64
 RADIX = 16
 FOLD = L // RADIX
+ODD = 7 * 2 * FOLD
 MESH = pl.DeviceIdType.MESH
 
 
@@ -73,10 +74,11 @@
     angle = 2 * math.pi * ((bins[..., None] * shifts) % L) / L
     lag = np.stack([np.cos(angle), -np.sin(angle)], axis=3)
     lag = lag.transpose(2, 3, 1, 0, 4).reshape(2 * BANDS, LAGS).T * float(WIN * BANDS) ** (-0.5)
-    odd = np.stack(split(odd.reshape(7, 128, 2 * FOLD)), axis=1)
-    even = np.stack(split(even.reshape(2, 64, FOLD)), axis=1)
-    lag = np.concatenate(split(lag), axis=0)
-    return odd, even, lag
+    odd = np.concatenate(split(odd.reshape(7, 128, 2 * FOLD).transpose(0, 2, 1)), axis=2).reshape(ODD, 256)
+    even = np.concatenate(split(even.reshape(2, 64, FOLD).transpose(0, 2, 1)), axis=2)
+    even = even.transpose(1, 0, 2).reshape(FOLD, 256)
+    lag = np.concatenate(split(lag), axis=0).reshape(2 * LAGS, 4, 256).transpose(1, 0, 2).reshape(8 * LAGS, 256)
+    return np.concatenate([odd, even, lag], axis=0)
 
 
 def fold16(x):
@@ -106,10 +108,10 @@
 
 
 def kernel(
-    x_ref, pair_ref, odd_ref, even_ref, lag_ref, out_ref,
+    x_ref, pair_ref, table_ref, out_ref,
     x_v, odd_v, even_v, lag_v, pairs, fodd, feven, spec, rows, codes, order,
     asend, arecv, bands, csend, crecv,
-    x_sem, t_sem, send_sem, p_sem, a_sem, c_sem,
+    x_sem, t_sem, send_sem, p_sem, a_sem, c_sem, ready_sem,
 ):
     me_s = lax.axis_index("sta")
     me_w = lax.axis_index("win")
@@ -119,9 +121,11 @@
         pltpu.make_async_copy(x_ref.at[pl.ds(2048 * i, 2048)], x_v.at[pl.ds(2048 * i, 2048)], x_sem.at[i])
         for i in range(4)
     ]
+    pieces = [(odd_v.at[pl.ds(1024 * q, 1024)], 1024 * q) for q in range(7)]
+    pieces += [(even_v, ODD), (lag_v, ODD + FOLD)]
     t_copies = [
-        pltpu.make_async_copy(src, dst, t_sem.at[i])
-        for i, (src, dst) in enumerate(((odd_ref, odd_v), (even_ref, even_v), (lag_ref, lag_v)))
+        pltpu.make_async_copy(table_ref.at[pl.ds(first, dst.shape[0])], dst, t_sem.at[i])
+        for i, (dst, first) in enumerate(pieces)
     ]
     for copy in x_copies + t_copies:
         copy.start()
@@ -144,10 +148,18 @@
 
     barrier = pltpu.get_barrier_semaphore()
 
-    def greet(z, w):
-        pl.semaphore_signal(barrier, inc=1, device_id={"sta": z, "win": w}, device_id_type=MESH)
-
-    to_others(greet)
+    def to_columns(action):
+        for offsets in FAR_FIRST[:-1]:
+            for offset in offsets:
+                action(column(offset))
+
+    def greet(i, _):
+        peer = lax.rem(me_w + i, WIN)
+        pl.semaphore_signal(barrier, inc=1, device_id={"win": peer}, device_id_type=MESH)
+        return 0
+
+    lax.fori_loop(1, WIN, greet, 0)
+    to_columns(lambda z: pl.semaphore_signal(barrier, inc=1, device_id={"sta": z}, device_id_type=MESH))
 
     def send(src, dst, phase, recv_sem, z, w):
         pltpu.make_async_remote_copy(
@@ -185,24 +197,23 @@
 
         lax.fori_loop(0, 8, fold, 0)
 
-    contract_last = (((1,), (1,)), ((), ()))
-
-    def dft(table, data):
-        high = lax.dot_general(table[0], data, contract_last, preferred_element_type=jnp.float32)
-        low = lax.dot_general(table[1], data[:ST], contract_last, preferred_element_type=jnp.float32)
-        return high[:, :ST] + (high[:, ST:] + low)
-
-    t_copies[0].wait()
-
-    def odd_class(q, power):
-        value = dft(odd_v[q], fodd[q])
-        spec[pl.ds(pl.multiple_of(q * 128, 128), 128), :] = value
-        return power + jnp.sum((value * value).reshape(16, 8, ST), axis=0)
-
-    power = lax.fori_loop(0, 7, odd_class, jnp.zeros((8, ST), jnp.float32))
-    t_copies[1].wait()
+    pl.semaphore_wait(barrier, STA - 1 + WIN - 1)
+    to_columns(lambda z: pl.semaphore_signal(ready_sem, inc=1, device_id={"sta": z}, device_id_type=MESH))
+
+    def dft(data, table):
+        prod = jnp.dot(data, table, preferred_element_type=jnp.float32)
+        bins = prod.shape[1] // 2
+        return jnp.transpose(prod[:ST, :bins] + (prod[:ST, bins:] + prod[ST:, :bins]))
+
+    power = jnp.zeros((8, ST), jnp.float32)
+    for q in range(7):
+        t_copies[q].wait()
+        value = dft(fodd[q], odd_v[1024 * q : 1024 * q + 1024])
+        spec[128 * q : 128 * q + 128, :] = value
+        power = power + jnp.sum((value * value).reshape(16, 8, ST), axis=0)
+    t_copies[7].wait()
     for half in range(2):
-        value = dft(even_v[half], feven[half])
+        value = dft(feven[half], even_v[:, 128 * half : 128 * half + 128])
         spec[896 + 64 * half : 960 + 64 * half, :] = value
         power = power + jnp.sum((value * value).reshape(8, 8, ST), axis=0)
     mean = jnp.sum(power, axis=0, keepdims=True) * (1.0 / BANDS)
@@ -211,12 +222,10 @@
         white = (spec[32 * i : 32 * i + 32, :] * inverse).astype(jnp.bfloat16)
         asend[8 * i : 8 * i + 8] = white.reshape(8, 4, ST)
 
-    pl.semaphore_wait(barrier, ALL - 1)
+    pl.semaphore_wait(ready_sem, STA - 1)
 
     to_others(lambda z, w: send(asend.at[w * STA + z], arecv.at[me], 0, a_sem, z, w))
-    for offsets in FAR_FIRST[:-1]:
-        for offset in offsets:
-            send(pair_ref, pairs.at[me_s], 2, p_sem, column(offset), me_w)
+    to_columns(lambda z: send(pair_ref, pairs.at[me_s], 2, p_sem, z, me_w))
     arecv[me] = asend[me_w * STA + me_s]
     pairs[me_s, 0, 0] = pair_ref[0, 0]
     pairs[me_s, 0, 1] = pair_ref[0, 1]
@@ -280,7 +289,7 @@
             lax.fori_loop(0, WIN if offset else WIN - 1, step, 0)
     crecv[me] = csend[me]
 
-    t_copies[2].wait()
+    t_copies[8].wait()
     wait(asend.at[pl.ds(0, ALL - 1)], send_sem.at[0])
     wait(pairs.at[pl.ds(0, STA - 1)], send_sem.at[2])
     wait(crecv.at[pl.ds(0, ALL - 1)], c_sem)
@@ -298,8 +307,15 @@
 
     def lags(t, _):
         row = pl.multiple_of(t * 128, 128)
-        value = jnp.dot(lag_v[pl.ds(row, 128), :], both, preferred_element_type=jnp.float32)
-        extra = jnp.dot(lag_v[pl.ds(row + LAGS, 128), :], high, preferred_element_type=jnp.float32)
+        value = jnp.zeros((128, 2 * ST), jnp.float32)
+        extra = jnp.zeros((128, ST), jnp.float32)
+        for block in range(4):
+            first = 2 * LAGS * block
+            part = both[256 * block : 256 * block + 256]
+            value += jnp.dot(lag_v[pl.ds(first + row, 128), :], part, preferred_element_type=jnp.float32)
+            extra += jnp.dot(
+                lag_v[pl.ds(first + LAGS + row, 128), :], part[:, :ST], preferred_element_type=jnp.float32
+            )
         value = jnp.transpose(value[:, :ST] + (value[:, ST:] + extra))
         for i2 in range(2):
             for j2 in range(2):
@@ -313,19 +329,19 @@
 
 
 def body(traces, pair_blocks):
-    odd, even, lag = (jnp.asarray(t) for t in tables())
+    table = jnp.asarray(tables())
     f32, bf16, i16 = jnp.float32, jnp.bfloat16, jnp.int16
     hbm = pl.BlockSpec(memory_space=pltpu.HBM)
     out = pl.pallas_call(
         kernel,
         out_shape=jax.ShapeDtypeStruct((2, 64, LAGS), f32),
-        in_specs=[hbm, pl.BlockSpec(memory_space=pltpu.SMEM), hbm, hbm, hbm],
+        in_specs=[hbm, pl.BlockSpec(memory_space=pltpu.SMEM), hbm],
         out_specs=pl.BlockSpec(memory_space=pltpu.VMEM),
         scratch_shapes=[
             pltpu.VMEM((ST * SEG, 128), f32),
-            pltpu.VMEM(odd.shape, bf16),
-            pltpu.VMEM(even.shape, bf16),
-            pltpu.VMEM(lag.shape, bf16),
+            pltpu.VMEM((ODD, 256), bf16),
+            pltpu.VMEM((FOLD, 256), bf16),
+            pltpu.VMEM((8 * LAGS, 256), bf16),
             pltpu.SMEM((STA, 1, 2), jnp.int32),
             pltpu.VMEM((7, 2 * ST, 2 * FOLD), bf16),
             pltpu.VMEM((2, 2 * ST, FOLD), bf16),
@@ -339,17 +355,18 @@
             pltpu.VMEM((ALL, 4, ST), i16),
             pltpu.VMEM((ALL, 4, ST), i16),
             pltpu.SemaphoreType.DMA((4,)),
-            pltpu.SemaphoreType.DMA((3,)),
+            pltpu.SemaphoreType.DMA((9,)),
             pltpu.SemaphoreType.DMA((3,)),
             pltpu.SemaphoreType.DMA,
             pltpu.SemaphoreType.DMA,
             pltpu.SemaphoreType.DMA,
+            pltpu.SemaphoreType.REGULAR,
         ],
         compiler_params=pltpu.CompilerParams(
-            collective_id=0, has_side_effects=True, vmem_limit_bytes=48 * 1024 * 1024
+            collective_id=0, has_side_effects=True, vmem_limit_bytes=58 * 1024 * 1024
         ),
         name="noise_correlation",
-    )(traces.reshape(ST * SEG, 128), pair_blocks, odd, even, lag)
+    )(traces.reshape(ST * SEG, 128), pair_blocks, table)
     return out.reshape(2, 1, 64, LAGS)
 
 

time: 44.5 us -> 43.1 us (0.969)
  local copies, waits for them, and re-layouts: 3.9 us -> 1.67 us
  Pallas kernels: 40.5 us -> 41.3 us
    unnamed x7 -> x1, local copies, waits for them, and re-layouts: 3.9 us -> 1.67 us
    pallas_call x1, Pallas kernels: 40.5 us -> 41.3 us  [body(): pl.pallas_call(kernel, out_shape=jax.ShapeDtypeStruct((2, 64, LAGS), f32)...]
where the time goes in v4:
time: 43.1 us; the launch traced here: 43 us
  Pallas kernels  41.3 us (96%)
  local copies, waits for them, and re-layouts  1.67 us (4%)
    pallas_call x1, Pallas kernels, body(): pl.pallas_call(kernel, out_shape=jax.ShapeDtypeStruct((2, 64, LAGS), f32)...  41.3 us
    unnamed x1, local copies, waits for them, and re-layouts  1.67 us

profile of v4, /device:TPU:1, one launch (start us, length us, event | category | flops | bytes accessed | tf_op | source)
XLA Modules:
  0.0 43.0 jit_solution(11315940165320756937)
XLA Ops:
  0.0 41.3 %noise_correlation.1 = f32[2,64,512]{2,1,0:T(8,128)} custom-call(f32[8192,128]{1,0:T(8,128)} %bitcast.4, s32[1,2]{1,0:T(1,128)} %pair_ref.1, bf16[11776,256]{1,0:T(8,128)(2,1)} %constant.2.clone.table_ref), custom_call_target="tpu_custom_call" | custom-call | tf_op jit(solution)/shard_map/noise_correlation/pallas_call | solution.py:335
  41.3 1.7 %copy.6 = f32[2,1,64,512]{3,2,1,0:T(8,128)} copy(f32[2,1,64,512]{3,2,1,0:T(8,128)} %bitcast.5) | data formatting | bytes 524288

commit v5 on v4

--- a/solution.py
+++ b/solution.py
@@ -75,8 +75,7 @@
     lag = np.stack([np.cos(angle), -np.sin(angle)], axis=3)
     lag = lag.transpose(2, 3, 1, 0, 4).reshape(2 * BANDS, LAGS).T * float(WIN * BANDS) ** (-0.5)
     odd = np.concatenate(split(odd.reshape(7, 128, 2 * FOLD).transpose(0, 2, 1)), axis=2).reshape(ODD, 256)
-    even = np.concatenate(split(even.reshape(2, 64, FOLD).transpose(0, 2, 1)), axis=2)
-    even = even.transpose(1, 0, 2).reshape(FOLD, 256)
+    even = np.concatenate(split(even.reshape(128, FOLD).T), axis=1)
     lag = np.concatenate(split(lag), axis=0).reshape(2 * LAGS, 4, 256).transpose(1, 0, 2).reshape(8 * LAGS, 256)
     return np.concatenate([odd, even, lag], axis=0)
 
@@ -111,7 +110,7 @@
     x_ref, pair_ref, table_ref, out_ref,
     x_v, odd_v, even_v, lag_v, pairs, fodd, feven, spec, rows, codes, order,
     asend, arecv, bands, csend, crecv,
-    x_sem, t_sem, send_sem, p_sem, a_sem, c_sem, ready_sem,
+    x_sem, t_sem, send_sem, p_sem, a_sem, c_sem,
 ):
     me_s = lax.axis_index("sta")
     me_w = lax.axis_index("win")
@@ -121,11 +120,9 @@
         pltpu.make_async_copy(x_ref.at[pl.ds(2048 * i, 2048)], x_v.at[pl.ds(2048 * i, 2048)], x_sem.at[i])
         for i in range(4)
     ]
-    pieces = [(odd_v.at[pl.ds(1024 * q, 1024)], 1024 * q) for q in range(7)]
-    pieces += [(even_v, ODD), (lag_v, ODD + FOLD)]
     t_copies = [
         pltpu.make_async_copy(table_ref.at[pl.ds(first, dst.shape[0])], dst, t_sem.at[i])
-        for i, (dst, first) in enumerate(pieces)
+        for i, (first, dst) in enumerate(((0, odd_v), (ODD, even_v), (ODD + FOLD, lag_v)))
     ]
     for copy in x_copies + t_copies:
         copy.start()
@@ -148,18 +145,16 @@
 
     barrier = pltpu.get_barrier_semaphore()
 
-    def to_columns(action):
-        for offsets in FAR_FIRST[:-1]:
-            for offset in offsets:
-                action(column(offset))
-
-    def greet(i, _):
-        peer = lax.rem(me_w + i, WIN)
-        pl.semaphore_signal(barrier, inc=1, device_id={"win": peer}, device_id_type=MESH)
+    def greet(offset, i):
+        w = lax.rem(me_w + i, WIN)
+        pl.semaphore_signal(barrier, inc=1, device_id={"sta": column(offset), "win": w}, device_id_type=MESH)
+
+    def greet_early(i, _):
+        for offset in (4, 3, 5):
+            greet(offset, i)
         return 0
 
-    lax.fori_loop(1, WIN, greet, 0)
-    to_columns(lambda z: pl.semaphore_signal(barrier, inc=1, device_id={"sta": z}, device_id_type=MESH))
+    lax.fori_loop(0, WIN, greet_early, 0)
 
     def send(src, dst, phase, recv_sem, z, w):
         pltpu.make_async_remote_copy(
@@ -174,6 +169,10 @@
         x_copies[chunk].wait()
 
         def fold(t, _, chunk=chunk):
+            if chunk < 2:
+                for offset in (2, 6, 1, 7, 0):
+                    for i in range(2):
+                        greet(offset, 16 * chunk + 2 * t + i)
             lane_tile = lax.rem(t, 4)
             i2 = t // 4
             first = chunk * 2048 + i2 * 64
@@ -197,35 +196,33 @@
 
         lax.fori_loop(0, 8, fold, 0)
 
-    pl.semaphore_wait(barrier, STA - 1 + WIN - 1)
-    to_columns(lambda z: pl.semaphore_signal(ready_sem, inc=1, device_id={"sta": z}, device_id_type=MESH))
-
     def dft(data, table):
         prod = jnp.dot(data, table, preferred_element_type=jnp.float32)
-        bins = prod.shape[1] // 2
-        return jnp.transpose(prod[:ST, :bins] + (prod[:ST, bins:] + prod[ST:, :bins]))
-
+        return prod[:ST, :128] + (prod[:ST, 128:] + prod[ST:, :128])
+
+    t_copies[0].wait()
+    t_copies[1].wait()
     power = jnp.zeros((8, ST), jnp.float32)
-    for q in range(7):
-        t_copies[q].wait()
-        value = dft(fodd[q], odd_v[1024 * q : 1024 * q + 1024])
+    for q in range(8):
+        if q < 7:
+            value = dft(fodd[q], odd_v[1024 * q : 1024 * q + 1024])
+        else:
+            first_half = lax.broadcasted_iota(jnp.int32, (ST, 128), 1) < 64
+            value = jnp.where(first_half, dft(feven[0], even_v[...]), dft(feven[1], even_v[...]))
+        value = jnp.transpose(value)
         spec[128 * q : 128 * q + 128, :] = value
         power = power + jnp.sum((value * value).reshape(16, 8, ST), axis=0)
-    t_copies[7].wait()
-    for half in range(2):
-        value = dft(feven[half], even_v[:, 128 * half : 128 * half + 128])
-        spec[896 + 64 * half : 960 + 64 * half, :] = value
-        power = power + jnp.sum((value * value).reshape(8, 8, ST), axis=0)
     mean = jnp.sum(power, axis=0, keepdims=True) * (1.0 / BANDS)
     inverse = 1.0 / jnp.sqrt(mean + 1e-06)
     for i in range(ALL // 8):
         white = (spec[32 * i : 32 * i + 32, :] * inverse).astype(jnp.bfloat16)
         asend[8 * i : 8 * i + 8] = white.reshape(8, 4, ST)
 
-    pl.semaphore_wait(ready_sem, STA - 1)
+    pl.semaphore_wait(barrier, ALL)
 
     to_others(lambda z, w: send(asend.at[w * STA + z], arecv.at[me], 0, a_sem, z, w))
-    to_columns(lambda z: send(pair_ref, pairs.at[me_s], 2, p_sem, z, me_w))
+    for offset in range(1, STA):
+        send(pair_ref, pairs.at[me_s], 2, p_sem, column(offset), me_w)
     arecv[me] = asend[me_w * STA + me_s]
     pairs[me_s, 0, 0] = pair_ref[0, 0]
     pairs[me_s, 0, 1] = pair_ref[0, 1]
@@ -289,7 +286,7 @@
             lax.fori_loop(0, WIN if offset else WIN - 1, step, 0)
     crecv[me] = csend[me]
 
-    t_copies[8].wait()
+    t_copies[2].wait()
     wait(asend.at[pl.ds(0, ALL - 1)], send_sem.at[0])
     wait(pairs.at[pl.ds(0, STA - 1)], send_sem.at[2])
     wait(crecv.at[pl.ds(0, ALL - 1)], c_sem)
@@ -355,12 +352,11 @@
             pltpu.VMEM((ALL, 4, ST), i16),
             pltpu.VMEM((ALL, 4, ST), i16),
             pltpu.SemaphoreType.DMA((4,)),
-            pltpu.SemaphoreType.DMA((9,)),
+            pltpu.SemaphoreType.DMA((3,)),
             pltpu.SemaphoreType.DMA((3,)),
             pltpu.SemaphoreType.DMA,
             pltpu.SemaphoreType.DMA,
             pltpu.SemaphoreType.DMA,
-            pltpu.SemaphoreType.REGULAR,
         ],
         compiler_params=pltpu.CompilerParams(
             collective_id=0, has_side_effects=True, vmem_limit_bytes=58 * 1024 * 1024

time: 43.1 us -> 41.7 us (0.968)
  Pallas kernels: 41.3 us -> 40 us
    pallas_call x1, Pallas kernels: 41.3 us -> 40 us  [body(): pl.pallas_call(kernel, out_shape=jax.ShapeDtypeStruct((2, 64, LAGS), f32)...]
where the time goes in v5:
time: 41.7 us; the launch traced here: 41.6 us
  Pallas kernels  40 us (96%)
  local copies, waits for them, and re-layouts  1.67 us (4%)
    pallas_call x1, Pallas kernels, body(): pl.pallas_call(kernel, out_shape=jax.ShapeDtypeStruct((2, 64, LAGS), f32)...  40 us
    unnamed x1, local copies, waits for them, and re-layouts  1.67 us

profile of v5, /device:TPU:1, one launch (start us, length us, event | category | flops | bytes accessed | tf_op | source)
XLA Modules:
  0.0 41.6 jit_solution(14740096141874600310)
XLA Ops:
  0.0 40.0 %noise_correlation.1 = f32[2,64,512]{2,1,0:T(8,128)} custom-call(f32[8192,128]{1,0:T(8,128)} %bitcast.4, s32[1,2]{1,0:T(1,128)} %pair_ref.1, bf16[11776,256]{1,0:T(8,128)(2,1)} %constant.2.clone.table_ref), custom_call_target="tpu_custom_call" | custom-call | tf_op jit(solution)/shard_map/noise_correlation/pallas_call | solution.py:332
  40.0 1.7 %copy.6 = f32[2,1,64,512]{3,2,1,0:T(8,128)} copy(f32[2,1,64,512]{3,2,1,0:T(8,128)} %bitcast.5) | data formatting | bytes 524288

commit v6 on v5

--- a/solution.py
+++ b/solution.py
@@ -74,8 +74,8 @@
     angle = 2 * math.pi * ((bins[..., None] * shifts) % L) / L
     lag = np.stack([np.cos(angle), -np.sin(angle)], axis=3)
     lag = lag.transpose(2, 3, 1, 0, 4).reshape(2 * BANDS, LAGS).T * float(WIN * BANDS) ** (-0.5)
-    odd = np.concatenate(split(odd.reshape(7, 128, 2 * FOLD).transpose(0, 2, 1)), axis=2).reshape(ODD, 256)
-    even = np.concatenate(split(even.reshape(128, FOLD).T), axis=1)
+    odd = np.concatenate(split(odd.transpose(0, 3, 1, 2, 4, 5).reshape(7, 128, 2 * FOLD).transpose(0, 2, 1)), axis=2).reshape(ODD, 256)
+    even = np.concatenate(split(even.transpose(3, 0, 1, 2, 4, 5).reshape(128, FOLD).T), axis=1)
     lag = np.concatenate(split(lag), axis=0).reshape(2 * LAGS, 4, 256).transpose(1, 0, 2).reshape(8 * LAGS, 256)
     return np.concatenate([odd, even, lag], axis=0)
 
@@ -108,13 +108,15 @@
 
 def kernel(
     x_ref, pair_ref, table_ref, out_ref,
-    x_v, odd_v, even_v, lag_v, pairs, fodd, feven, spec, rows, codes, order,
-    asend, arecv, bands, csend, crecv,
+    x_v, odd_v, even_v, lag_v, pairs, fodd, feven, spec, rows, bands, codes, total, order,
+    asend_0, asend_1, arecv_0, arecv_1, csend_0, csend_1, crecv_0, crecv_1,
     x_sem, t_sem, send_sem, p_sem, a_sem, c_sem,
 ):
     me_s = lax.axis_index("sta")
     me_w = lax.axis_index("win")
     me = me_s * WIN + me_w
+    asend, arecv = (asend_0, asend_1), (arecv_0, arecv_1)
+    csend, crecv = (csend_0, csend_1), (crecv_0, crecv_1)
 
     x_copies = [
         pltpu.make_async_copy(x_ref.at[pl.ds(2048 * i, 2048)], x_v.at[pl.ds(2048 * i, 2048)], x_sem.at[i])
@@ -124,7 +126,7 @@
         pltpu.make_async_copy(table_ref.at[pl.ds(first, dst.shape[0])], dst, t_sem.at[i])
         for i, (first, dst) in enumerate(((0, odd_v), (ODD, even_v), (ODD + FOLD, lag_v)))
     ]
-    for copy in x_copies + t_copies:
+    for copy in x_copies + t_copies[:2]:
         copy.start()
 
     def column(offset):
@@ -202,127 +204,131 @@
 
     t_copies[0].wait()
     t_copies[1].wait()
+    t_copies[2].start()
     power = jnp.zeros((8, ST), jnp.float32)
     for q in range(8):
         if q < 7:
             value = dft(fodd[q], odd_v[1024 * q : 1024 * q + 1024])
         else:
-            first_half = lax.broadcasted_iota(jnp.int32, (ST, 128), 1) < 64
+            first_half = lax.rem(lax.broadcasted_iota(jnp.int32, (ST, 128), 1), 64) < 32
             value = jnp.where(first_half, dft(feven[0], even_v[...]), dft(feven[1], even_v[...]))
         value = jnp.transpose(value)
         spec[128 * q : 128 * q + 128, :] = value
         power = power + jnp.sum((value * value).reshape(16, 8, ST), axis=0)
     mean = jnp.sum(power, axis=0, keepdims=True) * (1.0 / BANDS)
     inverse = 1.0 / jnp.sqrt(mean + 1e-06)
-    for i in range(ALL // 8):
-        white = (spec[32 * i : 32 * i + 32, :] * inverse).astype(jnp.bfloat16)
-        asend[8 * i : 8 * i + 8] = white.reshape(8, 4, ST)
+    for q in range(8):
+        for s in range(2):
+            first = 128 * q + 64 * s
+            white = (spec[first : first + 64, :] * inverse).astype(jnp.bfloat16)
+            asend[s][32 * q : 32 * q + 32] = white.reshape(32, 2, ST)
 
     pl.semaphore_wait(barrier, ALL)
 
-    to_others(lambda z, w: send(asend.at[w * STA + z], arecv.at[me], 0, a_sem, z, w))
-    for offset in range(1, STA):
-        send(pair_ref, pairs.at[me_s], 2, p_sem, column(offset), me_w)
-    arecv[me] = asend[me_w * STA + me_s]
+    for s in range(2):
+        to_others(lambda z, w, s=s: send(asend[s].at[w * STA + z], arecv[s].at[me], s, a_sem.at[s], z, w))
+        if s == 0:
+            for offset in range(1, STA):
+                send(pair_ref, pairs.at[me_s], 4, p_sem, column(offset), me_w)
+        arecv[s][me] = asend[s][me_w * STA + me_s]
     pairs[me_s, 0, 0] = pair_ref[0, 0]
     pairs[me_s, 0, 1] = pair_ref[0, 1]
-    wait(arecv.at[pl.ds(0, ALL - 1)], a_sem)
-
-    for z in range(STA):
-        part = arecv[WIN * z : WIN * z + WIN].astype(jnp.float32)
-        rows[128 * z : 128 * z + 128, :] = part.reshape(4 * WIN, ST)
-    for z in range(STA):
-        for r in range(4):
-            part = rows[pl.ds(128 * z + r, WIN, stride=4), :]
-            bands[z, WIN * r : WIN * r + WIN, :] = part.astype(jnp.bfloat16)
-    wait(pairs.at[pl.ds(0, STA - 1)], p_sem)
 
     left_lanes = lax.broadcasted_iota(jnp.int32, (WIN, ST), 1) < 64
 
-    def cross(p):
+    def cross(p, s):
         a = pairs[p, 0, 0]
         b = pairs[p, 0, 1]
         a_odd = lax.rem(a, 2) == 1
         b_odd = lax.rem(b, 2) == 1
-        first = bands[a // 2]
-        second = bands[b // 2].astype(jnp.float32)
-        parts = []
-        for s in range(2):
-            re, im = second[64 * s : 64 * s + 32], second[64 * s + 32 : 64 * s + 64]
-            re_roll, im_roll = pltpu.roll(re, 64, 1), pltpu.roll(im, 64, 1)
-            re_l, im_l = jnp.where(b_odd, re_roll, re), jnp.where(b_odd, im_roll, im)
-            re_r, im_r = jnp.where(b_odd, re, re_roll), jnp.where(b_odd, im, im_roll)
-            right = jnp.concatenate(
-                [jnp.where(left_lanes, re_l, -im_r), jnp.where(left_lanes, im_l, re_r)], axis=0
-            ).astype(jnp.bfloat16)
-            left = first[64 * s : 64 * s + 64]
-            prod = lax.dot_general(left, right, (((0,), (0,)), ((), ())), preferred_element_type=jnp.float32)
-            prod = jnp.where(a_odd, prod[64:], prod[:64])
-            top, low = prod[:32], prod[32:]
-            parts.append(jnp.where(left_lanes, top, pltpu.roll(low, 64, 1)))
-            parts.append(jnp.where(left_lanes, pltpu.roll(top, 64, 1), low))
-        return parts
-
-    def encode(p, parts):
-        largest = functools.reduce(jnp.maximum, [jnp.abs(v) for v in parts])
+        left = bands[s, a // 2]
+        second = bands[s, b // 2].astype(jnp.float32)
+        re, im = second[:WIN], second[WIN:]
+        re_roll, im_roll = pltpu.roll(re, 64, 1), pltpu.roll(im, 64, 1)
+        re_l, im_l = jnp.where(b_odd, re_roll, re), jnp.where(b_odd, im_roll, im)
+        re_r, im_r = jnp.where(b_odd, re, re_roll), jnp.where(b_odd, im, im_roll)
+        right = jnp.concatenate(
+            [jnp.where(left_lanes, re_l, -im_r), jnp.where(left_lanes, im_l, re_r)], axis=0
+        ).astype(jnp.bfloat16)
+        prod = lax.dot_general(left, right, (((0,), (0,)), ((), ())), preferred_element_type=jnp.float32)
+        prod = jnp.where(a_odd, prod[64:], prod[:64])
+        top, low = prod[:32], prod[32:]
+        return jnp.where(left_lanes, top, pltpu.roll(low, 64, 1)), jnp.where(left_lanes, pltpu.roll(top, 64, 1), low)
+
+    def encode(p, s, parts):
+        largest = jnp.maximum(jnp.abs(parts[0]), jnp.abs(parts[1]))
         exponent = jnp.floor(jnp.log(jnp.maximum(largest, 1e-30)) * (1.0 / math.log(2.0))) + 1.0
-        scale = jnp.exp2(13.0 - exponent)
+        scale = jnp.exp2(11.0 - exponent)
         exponent = exponent.astype(jnp.int32) + 128
-        for r, v in enumerate(parts):
-            value = jnp.clip(jnp.round(v * scale), -8191.0, 8191.0).astype(jnp.int32)
-            codes[pl.ds(r, WIN, stride=4), :] = value * 4 + (jnp.right_shift(exponent, 2 * r) & 3)
-        csend[pl.ds(WIN * p, WIN)] = codes[:128, :].astype(jnp.int16).reshape(WIN, 4, ST)
-
-    for offsets in FAR_FIRST:
-        for offset in offsets:
-            p = column(offset)
-            encode(p, cross(p))
-
-            def step(i, _, p=p, offset=offset):
-                w = lax.rem(me_w + (20 if offset else 1) + i, WIN)
-                send(csend.at[p * WIN + w], crecv.at[me], 1, c_sem, p, w)
-                return 0
-
-            lax.fori_loop(0, WIN if offset else WIN - 1, step, 0)
-    crecv[me] = csend[me]
+        for c, v in enumerate(parts):
+            value = jnp.clip(jnp.round(v * scale), -2047.0, 2047.0).astype(jnp.int32)
+            codes[pl.ds(c, WIN, stride=2), :] = value * 16 + (jnp.right_shift(exponent, 4 * c) & 15)
+        csend[s][pl.ds(WIN * p, WIN)] = codes[:64, :].astype(jnp.int16).reshape(WIN, 2, ST)
+
+    for s in range(2):
+        wait(arecv[s].at[pl.ds(0, ALL - 1)], a_sem.at[s])
+        for z in range(STA):
+            part = arecv[s][WIN * z : WIN * z + WIN].astype(jnp.float32)
+            rows[64 * z : 64 * z + 64, :] = part.reshape(2 * WIN, ST)
+        for z in range(STA):
+            for c in range(2):
+                part = rows[pl.ds(64 * z + c, WIN, stride=2), :]
+                bands[s, z, WIN * c : WIN * c + WIN, :] = part.astype(jnp.bfloat16)
+        if s == 0:
+            wait(pairs.at[pl.ds(0, STA - 1)], p_sem)
+        for offsets in FAR_FIRST:
+            for offset in offsets:
+                p = column(offset)
+                encode(p, s, cross(p, s))
+
+                def step(i, _, p=p, offset=offset, s=s):
+                    w = lax.rem(me_w + (20 if offset else 1) + i, WIN)
+                    send(csend[s].at[p * WIN + w], crecv[s].at[me], 2 + s, c_sem.at[s], p, w)
+                    return 0
+
+                lax.fori_loop(0, WIN if offset else WIN - 1, step, 0)
+        crecv[s][me] = csend[s][me]
 
     t_copies[2].wait()
-    wait(asend.at[pl.ds(0, ALL - 1)], send_sem.at[0])
-    wait(pairs.at[pl.ds(0, STA - 1)], send_sem.at[2])
-    wait(crecv.at[pl.ds(0, ALL - 1)], c_sem)
-
-    for z in range(STA):
-        part = crecv[WIN * z : WIN * z + WIN].astype(jnp.int32)
-        codes[128 * z : 128 * z + 128, :] = part.reshape(4 * WIN, ST)
-    coded = [codes[pl.ds(r, ALL, stride=4), :] for r in range(4)]
-    exponent = functools.reduce(jnp.bitwise_or, [jnp.left_shift(v & 3, 2 * r) for r, v in enumerate(coded)])
-    scale = jnp.exp2((exponent - 141).astype(jnp.float32))
-    value = jnp.concatenate([jnp.right_shift(v, 2).astype(jnp.float32) * scale for v in coded], axis=0)
-    high = value.astype(jnp.bfloat16)
-    low = (value - high.astype(jnp.float32)).astype(jnp.bfloat16)
-    both = jnp.concatenate([high, low], axis=1)
-
-    def lags(t, _):
-        row = pl.multiple_of(t * 128, 128)
-        value = jnp.zeros((128, 2 * ST), jnp.float32)
-        extra = jnp.zeros((128, ST), jnp.float32)
-        for block in range(4):
-            first = 2 * LAGS * block
-            part = both[256 * block : 256 * block + 256]
-            value += jnp.dot(lag_v[pl.ds(first + row, 128), :], part, preferred_element_type=jnp.float32)
-            extra += jnp.dot(
-                lag_v[pl.ds(first + LAGS + row, 128), :], part[:, :ST], preferred_element_type=jnp.float32
-            )
-        value = jnp.transpose(value[:, :ST] + (value[:, ST:] + extra))
-        for i2 in range(2):
-            for j2 in range(2):
-                part = value[(2 * i2 + j2) * 32 : (2 * i2 + j2) * 32 + 32]
-                order[pl.ds(i2 * 64 + j2, 32, stride=2), :] = part
-        out_ref[:, :, pl.ds(row, 128)] = order[...].reshape(2, 64, 128)
-        return 0
-
-    lax.fori_loop(0, LAGS // 128, lags, 0)
-    wait(csend.at[pl.ds(0, ALL - 1)], send_sem.at[1])
+    wait(pairs.at[pl.ds(0, STA - 1)], send_sem.at[4])
+    for s in range(2):
+        wait(asend[s].at[pl.ds(0, ALL - 1)], send_sem.at[s])
+
+    for s in range(2):
+        wait(crecv[s].at[pl.ds(0, ALL - 1)], c_sem.at[s])
+        for z in range(STA):
+            part = crecv[s][WIN * z : WIN * z + WIN].astype(jnp.int32)
+            codes[64 * z : 64 * z + 64, :] = part.reshape(2 * WIN, ST)
+        coded = [codes[pl.ds(c, ALL, stride=2), :] for c in range(2)]
+        exponent = (coded[0] & 15) | jnp.left_shift(coded[1] & 15, 4)
+        scale = jnp.exp2((exponent - 139).astype(jnp.float32))
+        value = jnp.concatenate([jnp.right_shift(v, 4).astype(jnp.float32) * scale for v in coded], axis=0)
+        high = value.astype(jnp.bfloat16)
+        low = (value - high.astype(jnp.float32)).astype(jnp.bfloat16)
+        both = jnp.concatenate([high, low], axis=1)
+
+        for t in range(LAGS // 128):
+            row = 128 * t
+            value = jnp.zeros((128, 2 * ST), jnp.float32)
+            extra = jnp.zeros((128, ST), jnp.float32)
+            for block in range(2):
+                first = 2 * LAGS * (2 * s + block) + row
+                part = both[256 * block : 256 * block + 256]
+                value += jnp.dot(lag_v[first : first + 128, :], part, preferred_element_type=jnp.float32)
+                extra += jnp.dot(
+                    lag_v[first + LAGS : first + LAGS + 128, :], part[:, :ST], preferred_element_type=jnp.float32
+                )
+            value = value[:, :ST] + (value[:, ST:] + extra)
+            if s == 0:
+                total[row : row + 128, :] = value
+                continue
+            value = jnp.transpose(value + total[row : row + 128, :])
+            for i2 in range(2):
+                for j2 in range(2):
+                    part = value[(2 * i2 + j2) * 32 : (2 * i2 + j2) * 32 + 32]
+                    order[pl.ds(row + i2 * 64 + j2, 32, stride=2), :] = part
+            out_ref[:, :, row : row + 128] = order[row : row + 128, :].reshape(2, 64, 128)
+        wait(csend[s].at[pl.ds(0, ALL - 1)], send_sem.at[2 + s])
 
 
 def body(traces, pair_blocks):
@@ -343,23 +349,24 @@
             pltpu.VMEM((7, 2 * ST, 2 * FOLD), bf16),
             pltpu.VMEM((2, 2 * ST, FOLD), bf16),
             pltpu.VMEM((2 * BANDS, ST), f32),
-            pltpu.VMEM((2 * BANDS, ST), f32),
-            pltpu.VMEM((2 * BANDS, ST), jnp.int32),
-            pltpu.VMEM((ST, 128), f32),
-            pltpu.VMEM((ALL, 4, ST), bf16),
-            pltpu.VMEM((ALL, 4, ST), bf16),
-            pltpu.VMEM((STA, 4 * WIN, ST), bf16),
-            pltpu.VMEM((ALL, 4, ST), i16),
-            pltpu.VMEM((ALL, 4, ST), i16),
+            pltpu.VMEM((BANDS, ST), f32),
+            pltpu.VMEM((2, STA, 2 * WIN, ST), bf16),
+            pltpu.VMEM((BANDS, ST), jnp.int32),
+            pltpu.VMEM((LAGS, ST), f32),
+            pltpu.VMEM((LAGS, ST), f32),
+        ]
+        + [pltpu.VMEM((ALL, 2, ST), bf16)] * 4
+        + [pltpu.VMEM((ALL, 2, ST), i16)] * 4
+        + [
             pltpu.SemaphoreType.DMA((4,)),
             pltpu.SemaphoreType.DMA((3,)),
-            pltpu.SemaphoreType.DMA((3,)),
+            pltpu.SemaphoreType.DMA((5,)),
             pltpu.SemaphoreType.DMA,
-            pltpu.SemaphoreType.DMA,
-            pltpu.SemaphoreType.DMA,
+            pltpu.SemaphoreType.DMA((2,)),
+            pltpu.SemaphoreType.DMA((2,)),
         ],
         compiler_params=pltpu.CompilerParams(
-            collective_id=0, has_side_effects=True, vmem_limit_bytes=58 * 1024 * 1024
+            collective_id=0, has_side_effects=True, vmem_limit_bytes=54 * 1024 * 1024
         ),
         name="noise_correlation",
     )(traces.reshape(ST * SEG, 128), pair_blocks, table)

time: 41.7 us -> 42.2 us (1.012)
    pallas_call x1, Pallas kernels: 40 us -> 40.4 us  [body(): pl.pallas_call(kernel, out_shape=jax.ShapeDtypeStruct((2, 64, LAGS), f32)...]
where the time goes in v6:
time: 42.2 us; the launch traced here: 42.1 us
  Pallas kernels  40.4 us (96%)
  local copies, waits for them, and re-layouts  1.67 us (4%)
    pallas_call x1, Pallas kernels, body(): pl.pallas_call(kernel, out_shape=jax.ShapeDtypeStruct((2, 64, LAGS), f32)...  40.4 us
    unnamed x1, local copies, waits for them, and re-layouts  1.67 us

profile of v6, /device:TPU:1, one launch (start us, length us, event | category | flops | bytes accessed | tf_op | source)
XLA Modules:
  0.0 42.1 jit_solution(12566316646590965776)
XLA Ops:
  0.0 40.4 %noise_correlation.1 = f32[2,64,512]{2,1,0:T(8,128)} custom-call(f32[8192,128]{1,0:T(8,128)} %bitcast.4, s32[1,2]{1,0:T(1,128)} %pair_ref.1, bf16[11776,256]{1,0:T(8,128)(2,1)} %constant.2.clone.table_ref), custom_call_target="tpu_custom_call" | custom-call | tf_op jit(solution)/shard_map/noise_correlation/pallas_call | solution.py:338
  40.4 1.7 %copy.6 = f32[2,1,64,512]{3,2,1,0:T(8,128)} copy(f32[2,1,64,512]{3,2,1,0:T(8,128)} %bitcast.5) | data formatting | bytes 524288

commit v7 on v6

--- a/solution.py
+++ b/solution.py
@@ -277,16 +277,17 @@
         if s == 0:
             wait(pairs.at[pl.ds(0, STA - 1)], p_sem)
         for offsets in FAR_FIRST:
-            for offset in offsets:
-                p = column(offset)
+            pairs_now = [column(offset) for offset in offsets]
+            for p in pairs_now:
                 encode(p, s, cross(p, s))
 
-                def step(i, _, p=p, offset=offset, s=s):
-                    w = lax.rem(me_w + (20 if offset else 1) + i, WIN)
+            def step(i, _, pairs_now=pairs_now, here=0 in offsets, s=s):
+                w = lax.rem(me_w + (1 if here else 20) + i, WIN)
+                for p in pairs_now:
                     send(csend[s].at[p * WIN + w], crecv[s].at[me], 2 + s, c_sem.at[s], p, w)
-                    return 0
-
-                lax.fori_loop(0, WIN if offset else WIN - 1, step, 0)
+                return 0
+
+            lax.fori_loop(0, WIN - 1 if 0 in offsets else WIN, step, 0)
         crecv[s][me] = csend[s][me]
 
     t_copies[2].wait()
@@ -366,7 +367,7 @@
             pltpu.SemaphoreType.DMA((2,)),
         ],
         compiler_params=pltpu.CompilerParams(
-            collective_id=0, has_side_effects=True, vmem_limit_bytes=54 * 1024 * 1024
+            collective_id=0, has_side_effects=True, vmem_limit_bytes=52 * 1024 * 1024
         ),
         name="noise_correlation",
     )(traces.reshape(ST * SEG, 128), pair_blocks, table)

time: 42.2 us -> 38.2 us (0.905)
  Pallas kernels: 40.4 us -> 36.8 us
    pallas_call x1, Pallas kernels: 40.4 us -> 36.8 us  [body(): pl.pallas_call(kernel, out_shape=jax.ShapeDtypeStruct((2, 64, LAGS), f32)...]
    unnamed x1 -> x3, local copies, waits for them, and re-layouts: 1.67 us -> 1.36 us
where the time goes in v7:
time: 38.2 us
  Pallas kernels  36.8 us (96%)
  local copies, waits for them, and re-layouts  1.36 us (4%)
    pallas_call x1, Pallas kernels, body(): pl.pallas_call(kernel, out_shape=jax.ShapeDtypeStruct((2, 64, LAGS), f32)...  36.8 us
    unnamed x3, local copies, waits for them, and re-layouts  1.36 us

profile of v7, /device:TPU:1, one launch (start us, length us, event | category | flops | bytes accessed | tf_op | source)
XLA Modules:
  0.0 38.2 jit_solution(12170354031050309424)
XLA Ops:
  0.0 0.0 copy-start
  0.0 0.7 %copy-done = s32[1,2]{1,0:T(1,128)S(1)} copy-done((s32[1,2]{1,0:T(1,128)S(1)}, s32[1,2]{1,0:T(1,128)}, u32[]{:S(2)}) %copy-start) | copy-done | bytes 32
  0.7 36.8 %noise_correlation.1 = f32[2,64,512]{2,1,0:T(8,128)S(1)} custom-call(f32[8192,128]{1,0:T(8,128)} %bitcast.5, s32[1,2]{1,0:T(1,128)S(1)} %copy-done, bf16[11776,256]{1,0:T(8,128)(2,1)} %constant.2.clone.table_ref), custom_call_target="tpu_custom_call" | custom-call | tf_op jit(solution)/shard_map/noise_correlation/pallas_call | solution.py:339
  37.5 0.7 %copy.6 = f32[2,1,64,512]{3,2,1,0:T(8,128)} copy(f32[2,1,64,512]{3,2,1,0:T(8,128)S(1)} %bitcast.4) | data formatting | bytes 524288
Async XLA Ops:
  0.0 0.7 %copy-start = (s32[1,2]{1,0:T(1,128)S(1)}, s32[1,2]{1,0:T(1,128)}, u32[]{:S(2)}) copy-start(s32[1,2]{1,0:T(1,128)} %pair_ref.1) | copy-start | bytes 28

commit v8 on v7

--- a/solution.py
+++ b/solution.py
@@ -132,31 +132,37 @@
     def column(offset):
         return lax.rem(me_s + offset, STA)
 
+    row = me_w // 8
+    near = [lax.rem(lax.rem(me_w, 8) + i, 8) for i in (4, 5, 3, 2, 6, 7, 1, 0)]
+
+    def in_columns(offsets, action):
+        columns = [column(offset) for offset in offsets]
+
+        def step(i, _):
+            base = lax.rem(row + 2 + i, 4) * 8
+            for w in near:
+                for z in columns:
+                    action(z, base + w)
+            return 0
+
+        if 0 not in offsets:
+            lax.fori_loop(0, 4, step, 0)
+            return
+        lax.fori_loop(0, 2, step, 0)
+        lax.fori_loop(3, 4, step, 0)
+        for w in near[:-1]:
+            action(columns[0], row * 8 + w)
+
     def to_others(action):
-        def in_columns(offsets):
-            def step(i, _):
-                w = lax.rem(me_w + (1 if 0 in offsets else 20) + i, WIN)
-                for offset in offsets:
-                    action(column(offset), w)
-                return 0
-
-            lax.fori_loop(0, WIN - 1 if 0 in offsets else WIN, step, 0)
-
         for offsets in FAR_FIRST:
-            in_columns(offsets)
+            in_columns(offsets, action)
 
     barrier = pltpu.get_barrier_semaphore()
 
-    def greet(offset, i):
-        w = lax.rem(me_w + i, WIN)
-        pl.semaphore_signal(barrier, inc=1, device_id={"sta": column(offset), "win": w}, device_id_type=MESH)
-
-    def greet_early(i, _):
-        for offset in (4, 3, 5):
-            greet(offset, i)
-        return 0
-
-    lax.fori_loop(0, WIN, greet_early, 0)
+    def greet(z, w):
+        pl.semaphore_signal(barrier, inc=1, device_id={"sta": z, "win": w}, device_id_type=MESH)
+
+    to_others(greet)
 
     def send(src, dst, phase, recv_sem, z, w):
         pltpu.make_async_remote_copy(
@@ -171,10 +177,6 @@
         x_copies[chunk].wait()
 
         def fold(t, _, chunk=chunk):
-            if chunk < 2:
-                for offset in (2, 6, 1, 7, 0):
-                    for i in range(2):
-                        greet(offset, 16 * chunk + 2 * t + i)
             lane_tile = lax.rem(t, 4)
             i2 = t // 4
             first = chunk * 2048 + i2 * 64
@@ -217,15 +219,18 @@
         power = power + jnp.sum((value * value).reshape(16, 8, ST), axis=0)
     mean = jnp.sum(power, axis=0, keepdims=True) * (1.0 / BANDS)
     inverse = 1.0 / jnp.sqrt(mean + 1e-06)
-    for q in range(8):
-        for s in range(2):
+    def whiten(s):
+        for q in range(8):
             first = 128 * q + 64 * s
             white = (spec[first : first + 64, :] * inverse).astype(jnp.bfloat16)
             asend[s][32 * q : 32 * q + 32] = white.reshape(32, 2, ST)
 
-    pl.semaphore_wait(barrier, ALL)
+    whiten(0)
+    pl.semaphore_wait(barrier, ALL - 1)
 
     for s in range(2):
+        if s == 1:
+            whiten(1)
         to_others(lambda z, w, s=s: send(asend[s].at[w * STA + z], arecv[s].at[me], s, a_sem.at[s], z, w))
         if s == 0:
             for offset in range(1, STA):
@@ -281,13 +286,9 @@
             for p in pairs_now:
                 encode(p, s, cross(p, s))
 
-            def step(i, _, pairs_now=pairs_now, here=0 in offsets, s=s):
-                w = lax.rem(me_w + (1 if here else 20) + i, WIN)
-                for p in pairs_now:
-                    send(csend[s].at[p * WIN + w], crecv[s].at[me], 2 + s, c_sem.at[s], p, w)
-                return 0
-
-            lax.fori_loop(0, WIN - 1 if 0 in offsets else WIN, step, 0)
+            in_columns(
+                offsets, lambda p, w, s=s: send(csend[s].at[p * WIN + w], crecv[s].at[me], 2 + s, c_sem.at[s], p, w)
+            )
         crecv[s][me] = csend[s][me]
 
     t_copies[2].wait()

time: 38.2 us -> 35.4 us (0.927)
  Pallas kernels: 36.8 us -> 34 us
    pallas_call x1, Pallas kernels: 36.8 us -> 34 us  [body(): pl.pallas_call(kernel, out_shape=jax.ShapeDtypeStruct((2, 64, LAGS), f32)...]
where the time goes in v8:
time: 35.4 us; the launch traced here: 35.3 us
  Pallas kernels  34 us (96%)
  local copies, waits for them, and re-layouts  1.36 us (4%)
    pallas_call x1, Pallas kernels, body(): pl.pallas_call(kernel, out_shape=jax.ShapeDtypeStruct((2, 64, LAGS), f32)...  34 us
    unnamed x3, local copies, waits for them, and re-layouts  1.36 us

profile of v8, /device:TPU:1, one launch (start us, length us, event | category | flops | bytes accessed | tf_op | source)
XLA Modules:
  0.0 35.3 jit_solution(9039571663523964474)
XLA Ops:
  0.0 0.0 copy-start
  0.0 0.7 %copy-done = s32[1,2]{1,0:T(1,128)S(1)} copy-done((s32[1,2]{1,0:T(1,128)S(1)}, s32[1,2]{1,0:T(1,128)}, u32[]{:S(2)}) %copy-start) | copy-done | bytes 32
  0.7 34.0 %noise_correlation.1 = f32[2,64,512]{2,1,0:T(8,128)S(1)} custom-call(f32[8192,128]{1,0:T(8,128)} %bitcast.5, s32[1,2]{1,0:T(1,128)S(1)} %copy-done, bf16[11776,256]{1,0:T(8,128)(2,1)} %constant.2.clone.table_ref), custom_call_target="tpu_custom_call" | custom-call | tf_op jit(solution)/shard_map/noise_correlation/pallas_call | solution.py:340
  34.6 0.7 %copy.6 = f32[2,1,64,512]{3,2,1,0:T(8,128)} copy(f32[2,1,64,512]{3,2,1,0:T(8,128)S(1)} %bitcast.4) | data formatting | bytes 524288
Async XLA Ops:
  0.0 0.7 %copy-start = (s32[1,2]{1,0:T(1,128)S(1)}, s32[1,2]{1,0:T(1,128)}, u32[]{:S(2)}) copy-start(s32[1,2]{1,0:T(1,128)} %pair_ref.1) | copy-start | bytes 28

commit v9 on v8

--- a/solution.py
+++ b/solution.py
@@ -102,7 +102,7 @@
     return real, imag
 
 
-FAR_FIRST = ((4,), (3, 5), (2, 6), (1, 7), (0,))
+FAR_FIRST = ((4, 3, 5), (2, 6, 1, 7), (0,))
 ALL = STA * WIN
 
 

time: 35.4 us -> 35.2 us (level)
  no operation moved by 1% of the time
where the time goes in v9:
time: 35.2 us; the launch traced here: 35.1 us
  Pallas kernels  33.7 us (96%)
  local copies, waits for them, and re-layouts  1.36 us (4%)
    pallas_call x1, Pallas kernels, body(): pl.pallas_call(kernel, out_shape=jax.ShapeDtypeStruct((2, 64, LAGS), f32)...  33.7 us
    unnamed x3, local copies, waits for them, and re-layouts  1.36 us

profile of v9, /device:TPU:1, one launch (start us, length us, event | category | flops | bytes accessed | tf_op | source)
XLA Modules:
  0.0 35.1 jit_solution(12126995515341545417)
XLA Ops:
  0.0 0.0 copy-start
  0.0 0.7 %copy-done = s32[1,2]{1,0:T(1,128)S(1)} copy-done((s32[1,2]{1,0:T(1,128)S(1)}, s32[1,2]{1,0:T(1,128)}, u32[]{:S(2)}) %copy-start) | copy-done | bytes 32
  0.7 33.7 %noise_correlation.1 = f32[2,64,512]{2,1,0:T(8,128)S(1)} custom-call(f32[8192,128]{1,0:T(8,128)} %bitcast.5, s32[1,2]{1,0:T(1,128)S(1)} %copy-done, bf16[11776,256]{1,0:T(8,128)(2,1)} %constant.2.clone.table_ref), custom_call_target="tpu_custom_call" | custom-call | tf_op jit(solution)/shard_map/noise_correlation/pallas_call | solution.py:340
  34.4 0.7 %copy.6 = f32[2,1,64,512]{3,2,1,0:T(8,128)} copy(f32[2,1,64,512]{3,2,1,0:T(8,128)S(1)} %bitcast.4) | data formatting | bytes 524288
Async XLA Ops:
  0.0 0.7 %copy-start = (s32[1,2]{1,0:T(1,128)S(1)}, s32[1,2]{1,0:T(1,128)}, u32[]{:S(2)}) copy-start(s32[1,2]{1,0:T(1,128)} %pair_ref.1) | copy-start | bytes 28
